TPU v7x, 32 devices: a whole 2x2x4 slice. The times are simulated.
32 devices in a mesh: narrow: 8 (over z, y), wide: 4 (over x, core).
Axes of the slice: x: 2, y: 2, z: 4, core: 2. Of those that a mesh axis runs over, the one named last changes fastest.
Arguments:
- tokens: bfloat16 [2048, 2, 2048], P(('narrow', 'wide')), may hold values from -6 to 6
- lengths: int32 [2], replicated, may hold values from 64 to 2048, as said below
- attn_gain: float32 [2048], replicated, may hold values from 0.1 to 1.9
- w_query: bfloat16 [2048, 2048], P(None, 'wide'), may hold values from -0.125 to 0.125
- key_matrix: bfloat16 [2048, 512], P(None, 'wide'), may hold values from -0.125 to 0.125
- value_matrix: bfloat16 [2048, 512], P(None, 'wide'), may hold values from -0.125 to 0.125
- q_gain: float32 [64], replicated, may hold values from 0.1 to 1.9
- k_gain: float32 [64], replicated, may hold values from 0.1 to 1.9
- w_out: bfloat16 [2048, 2048], P('wide'), may hold values from -1 to 1
- ffn_gain: float32 [2048], replicated, may hold values from 0.1 to 1.9
- w_gate: bfloat16 [2048, 8192], P(None, 'wide'), may hold values from -0.125 to 0.125
- w_up: bfloat16 [2048, 8192], P(None, 'wide'), may hold values from -0.125 to 0.125
- w_down: bfloat16 [8192, 2048], P('wide'), may hold values from -0.0625 to 0.0625
- out_grad: bfloat16 [2048, 2, 2048], P(('narrow', 'wide')), may hold values from -6 to 6
Outputs:
- mixed: bfloat16 [2048, 2, 2048], P(('narrow', 'wide'))
- d_tokens: float32 [2048, 2, 2048], P(('narrow', 'wide'))
- d_attn_gain: float32 [2048], replicated
- d_w_query: float32 [2048, 2048], P('narrow', 'wide')
- d_w_key: float32 [2048, 512], P('narrow', 'wide')
- d_w_value: float32 [2048, 512], P('narrow', 'wide')
- d_q_gain: float32 [64], replicated
- d_k_gain: float32 [64], replicated
- d_w_out_t: float32 [2048, 2048], P('narrow', 'wide')
- d_ffn_gain: float32 [2048], replicated
- d_w_gate: float32 [2048, 8192], P('narrow', 'wide')
- d_w_up: float32 [2048, 8192], P('narrow', 'wide')
- d_w_down_t: float32 [2048, 8192], P('narrow', 'wide')
Inputs may be any that keep to these rules, and one draw needn't show every extreme that they name: `lengths`: in every draw one row, drawn from the seed, uses all 2048 slots; the others are mostly short.
All inputs are finite; a program needn't handle non-finite values.
Results may differ from a plain program's by a relative error of at most 0.02.
Values may be sent and summed in bfloat16 or wider, within the bound.
No kernel may reach another device: no remote copies, remote signals or barrier semaphores. Data moves between devices by JAX's collectives and lax.ppermute only.
A program may use at most 256 MiB of HBM per device.

v0:
```python
import functools
import math

import jax
import jax.numpy as jnp
from jax import lax
from jax.experimental import pallas as pl
from jax.experimental.pallas import tpu as pltpu
from jax.sharding import PartitionSpec as P

QUERY_HEADS = 32
KEY_VALUE_HEADS = 8
HEAD = 64
HALF = HEAD // 2
GROUP = QUERY_HEADS // KEY_VALUE_HEADS
EPS = 1e-06
SCALE = HEAD ** (-0.5)
AXES = ("narrow", "wide")
TP_BIT = 2
BF = jnp.bfloat16
F32 = jnp.float32
MIB = 2**20
KERNEL_FLOPS = 5 * 10**9

NN = (((1,), (0,)), ((), ()))
NT = (((1,), (1,)), ((), ()))
TN = (((0,), (0,)), ((), ()))


def mm(a, b, dims=NN):
    return lax.dot_general(a, b, dims, preferred_element_type=F32)


class Line:
    def __init__(self, at):
        self.at = at
        self.last = []
        self.needed = []

    def wait(self, *arrays):
        self.needed += arrays

    def call(self, kernel, *args, grid, in_specs, out_specs, out_shape, scratch=(), name=None, limit=52 * 2**20):
        extra = [*self.last, *self.needed]
        self.needed = []

        def body(at_ref, *refs):
            kernel(at_ref, *refs[len(extra) :])

        outs = pl.pallas_call(
            body,
            grid_spec=pltpu.PrefetchScalarGridSpec(
                num_scalar_prefetch=1,
                grid=grid,
                in_specs=[pl.BlockSpec(memory_space=pl.ANY)] * len(extra) + list(in_specs),
                out_specs=out_specs,
                scratch_shapes=scratch,
            ),
            out_shape=out_shape,
            compiler_params=pltpu.CompilerParams(vmem_limit_bytes=limit),
            cost_estimate=pl.CostEstimate(flops=KERNEL_FLOPS, bytes_accessed=0, transcendentals=0),
            name=name,
        )(self.at, *extra, *args)
        self.last = [outs[0] if isinstance(outs, (list, tuple)) else outs]
        return outs

    def small(self, kernel, *args, out_shape, name):
        spec = pl.BlockSpec(memory_space=pltpu.VMEM)
        outs = jax.tree.map(lambda _: spec, out_shape)
        return self.call(
            kernel, *args,
            grid=(), in_specs=[spec] * len(args), out_specs=outs, out_shape=out_shape, limit=8 * MIB, name=name,
        )


def position_inside(t, share, w):
    u = t // share
    return (((u & 1) << 1) | ((u >> 1) ^ (w & 1))) * share + t % share


def block_of(n, mask, i):
    return ((n ^ mask) & ~TP_BIT) | (TP_BIT * i)


def join(ref):
    return jnp.concatenate([ref[0, 0], ref[1, 0]], axis=0)


def split(ref, value):
    share = ref.shape[2]
    ref[0, 0] = value[:share]
    ref[1, 0] = value[share:]


def positions_in_block(size, share, w, axis):
    shape = (size, 1) if axis == 0 else (1, size)
    return position_inside(lax.broadcasted_iota(jnp.int32, shape, axis), share, w)


def constant(shape):
    return pl.BlockSpec(shape, lambda *_: (0,) * len(shape))


def per_block(shape):
    return pl.BlockSpec(shape, lambda g, i, at: (g, i) + (0,) * (len(shape) - 2))


def chips(share, columns):
    return pl.BlockSpec((2, 1, share, columns), lambda g, i, at: (i, g, 0, 0))


def per_sequence(shape):
    return pl.BlockSpec(shape, lambda g, *_: (g,) + (0,) * (len(shape) - 1))


def shape_of(shape, dtype=BF):
    return jax.ShapeDtypeStruct(shape, dtype)


def project_kernel(at_ref, a_ref, b_ref, wt_ref, cos_ref, sin_ref, qg_ref, kg_ref, kv_ref, q_ref, raw_ref):
    x = jnp.concatenate([join(a_ref), join(b_ref)], axis=0)
    y = mm(wt_ref[...], x, NT)
    heads = y.shape[0] // HEAD - 2
    width = heads * HEAD
    raw_ref[0, 0] = y[: width + HEAD]
    c, s = cos_ref[0], sin_ref[0]

    def norm_rope(v, gain):
        r = lax.rsqrt(jnp.mean(v * v, axis=0, keepdims=True) + EPS)
        n = v * r * gain
        a, b = n[:HALF], n[HALF:]
        return a * c - b * s, b * c + a * s

    q = []
    for h in range(heads):
        a, b = norm_rope(y[h * HEAD : (h + 1) * HEAD], qg_ref[...])
        q.append(jnp.concatenate([a, b], axis=0) * SCALE)
    q_ref[0, 0] = jnp.concatenate(q, axis=1).astype(BF)
    a, b = norm_rope(y[width : width + HEAD], kg_ref[...])
    kv = jnp.concatenate([a, b, y[width + HEAD :]], axis=0)
    kv_ref[0] = kv.T.astype(BF)


def project(line, xn, wt, cos, sin, q_gain, k_gain):
    _, g, share, m = xn[0].shape
    b = 4 * share
    c = wt.shape[0]
    heads = c // HEAD - 2
    table = pl.BlockSpec((1, HALF, b), lambda g, i, at: (i, 0, 0))
    return line.call(
        project_kernel, *xn, wt, cos, sin, q_gain, k_gain,
        grid=(g, 2),
        in_specs=[chips(share, m)] * 2
        + [constant((c, m)), table, table, constant((HEAD, 1)), constant((HEAD, 1))],
        out_specs=[
            per_block((1, b, 2 * HEAD)),
            per_block((1, 1, HEAD, heads * b)),
            per_block((1, 1, (heads + 1) * HEAD, b)),
        ],
        out_shape=[
            shape_of((g, 2 * b, 2 * HEAD)),
            shape_of((g, 2, HEAD, heads * b)),
            shape_of((g, 2, (heads + 1) * HEAD, b), F32),
        ],
        name="project",
    )


def attend_kernel(masks, share, at_ref, q_ref, *refs):
    kv_refs = refs[: len(masks)]
    wo_ref, pb_ref, pa_ref, oa_ref, ob_ref, log_ref, acc_ref = refs[len(masks) :]
    n, w = at_ref[0], at_ref[1]
    length = at_ref[3 + pl.program_id(0)]
    b = kv_refs[0].shape[1] // 2
    heads = q_ref.shape[3] // b
    nq = block_of(n, 0, pl.program_id(1))
    bound = jnp.minimum(nq * b + positions_in_block(b, share, w, 1), length - 1)
    bound = jnp.concatenate([bound] * heads, axis=1)
    acc_ref[...] = jnp.zeros_like(acc_ref)
    inside = positions_in_block(b, share, w, 0)
    low = lax.broadcasted_iota(jnp.int32, (b, 2 * HEAD), 1) < HEAD

    for k, kv_ref in enumerate(kv_refs):
        for tp in range(2):
            nk = block_of(n, masks[k], tp)

            def add(masked):
                kv = kv_ref[0, tp * b : (tp + 1) * b, :]
                p = jnp.exp(mm(kv[:, :HEAD], q_ref[0, 0]))
                if masked:
                    p = jnp.where(nk * b + inside <= bound, p, 0.0)
                acc_ref[...] += mm(jnp.where(low, jnp.ones_like(kv), kv), p.astype(BF), TN)

            whole = (nk < nq) & ((nk + 1) * b <= length)
            pl.when(whole)(functools.partial(add, False))
            pl.when((nk <= nq) & (nk * b < length) & jnp.logical_not(whole))(functools.partial(add, True))

    total = acc_ref[:1, :]
    log_ref[0, 0] = jnp.log(total)
    o = acc_ref[HEAD:, :] / total
    o = jnp.concatenate([o[:, h * b : (h + 1) * b] for h in range(heads)], axis=0).T.astype(BF)
    split(oa_ref, o[: b // 2])
    split(ob_ref, o[b // 2 :])
    part = mm(o, wo_ref[...]).astype(BF)
    split(pa_ref, part[: b // 2])
    split(pb_ref, part[b // 2 :])


def attend(line, q, kvs, masks, w_out, share):
    g, b = q.shape[0], kvs[0].shape[1] // 2
    heads = q.shape[3] // b
    m = w_out.shape[1]
    width = heads * HEAD
    return line.call(
        functools.partial(attend_kernel, masks, share), q, *kvs, w_out,
        grid=(g, 2),
        in_specs=[per_block((1, 1, HEAD, heads * b))]
        + [per_sequence((1, 2 * b, 2 * HEAD))] * len(kvs)
        + [pl.BlockSpec((width, m), lambda g, i, at: (at[2], 0))],
        out_specs=[chips(share, m)] * 2
        + [chips(share, width)] * 2
        + [per_block((1, 1, 1, heads * b))],
        out_shape=[shape_of((4, g, share, m))] * 2
        + [shape_of((4, g, share, width))] * 2
        + [shape_of((g, 2, 1, heads * b), F32)],
        scratch=[pltpu.VMEM((2 * HEAD, heads * b), F32)],
        name="attend",
    )


def attend_back_kernel(masks, share, at_ref, dha_ref, dhb_ref, q_ref, *refs):
    count = len(masks)
    kv_refs, refs = refs[:count], refs[count:]
    wo_ref, oa_ref, ob_ref, log_ref, raw_ref, cos_ref, sin_ref, qg_ref, dqa_ref, dqb_ref = refs[:10]
    dkv_refs, dqg_ref = refs[10 : 10 + count], refs[10 + count]
    q_ext, do_ext, delta, dq_acc, dkv_acc = refs[11 + count :]
    n, w = at_ref[0], at_ref[1]
    at_g, i = pl.program_id(0), pl.program_id(1)
    length = at_ref[3 + at_g]
    b = kv_refs[0].shape[1] // 2
    heads = q_ref.shape[3] // b
    nq = block_of(n, 0, i)
    bound = jnp.minimum(nq * b + positions_in_block(b, share, w, 1), length - 1)
    bound = jnp.concatenate([bound] * heads, axis=1)
    inside = positions_in_block(b, share, w, 0)

    @pl.when(i == 0)
    def _():
        dkv_acc[...] = jnp.zeros_like(dkv_acc)

    @pl.when((i == 0) & (at_g == 0))
    def _():
        dqg_ref[...] = jnp.zeros_like(dqg_ref)

    dq_acc[...] = jnp.zeros_like(dq_acc)

    @pl.when(nq * b < length)
    def _():
        dh = jnp.concatenate([join(dha_ref), join(dhb_ref)], axis=0)
        do = mm(wo_ref[...], dh, NT).astype(BF).astype(F32)
        o = jnp.concatenate([join(oa_ref), join(ob_ref)], axis=0).astype(F32).T

        def heads_side_by_side(x):
            return jnp.concatenate([x[h * HEAD : (h + 1) * HEAD] for h in range(heads)], axis=1)

        do = heads_side_by_side(do)
        delta[...] = jnp.sum(do * heads_side_by_side(o), axis=0, keepdims=True)
        none = jnp.zeros((HEAD, heads * b), BF)
        do_ext[...] = jnp.concatenate([none, do.astype(BF)], axis=0)
        q_ext[...] = jnp.concatenate([q_ref[0, 0], none], axis=0)

    for k, kv_ref in enumerate(kv_refs):
        for tp in range(2):
            nk = block_of(n, masks[k], tp)

            def add(masked):
                kv = kv_ref[0, tp * b : (tp + 1) * b, :]
                p = jnp.exp(mm(kv, q_ext[...]) - log_ref[0, 0])
                if masked:
                    p = jnp.where(nk * b + inside <= bound, p, 0.0)
                ds = (p * (mm(kv, do_ext[...]) - delta[...])).astype(BF)
                dq_acc[...] += mm(kv, ds, TN)
                rows = slice((2 * k + tp) * b, (2 * k + tp + 1) * b)
                dkv_acc[rows, :] += mm(ds, q_ext[...], NT) + mm(p.astype(BF), do_ext[...], NT)

            whole = (nk < nq) & ((nk + 1) * b <= length)
            seen = (nk <= nq) & (nk * b < length) & (nq * b < length)
            pl.when(seen & whole)(functools.partial(add, False))
            pl.when(seen & jnp.logical_not(whole))(functools.partial(add, True))

    c, s = cos_ref[0], sin_ref[0]
    parts = []
    gain_sum = jnp.zeros((HEAD, b), F32)
    for h in range(heads):
        dq = dq_acc[:HEAD, h * b : (h + 1) * b] * SCALE
        e1, e2 = dq[:HALF], dq[HALF:]
        e = jnp.concatenate([e1 * c + e2 * s, e2 * c - e1 * s], axis=0)
        v = raw_ref[0, 0, h * HEAD : (h + 1) * HEAD, :]
        r = lax.rsqrt(jnp.mean(v * v, axis=0, keepdims=True) + EPS)
        unit = v * r
        ge = qg_ref[...] * e
        parts.append(r * (ge - unit * jnp.mean(ge * unit, axis=0, keepdims=True)))
        gain_sum += e * unit
    dq = jnp.concatenate(parts, axis=0).T.astype(BF)
    split(dqa_ref, dq[: b // 2])
    split(dqb_ref, dq[b // 2 :])
    dqg_ref[...] += gain_sum

    @pl.when(i == 1)
    def _():
        for k, ref in enumerate(dkv_refs):
            ref[0] = dkv_acc[2 * k * b : 2 * (k + 1) * b, :].astype(BF)


def attend_back(line, dh, q, kvs, masks, w_out, o, log, raw, cos, sin, q_gain, share):
    g, b = q.shape[0], kvs[0].shape[1] // 2
    heads = q.shape[3] // b
    m = w_out.shape[1]
    width = heads * HEAD
    half_rows = chips(share, width)
    table = pl.BlockSpec((1, HALF, b), lambda g, i, at: (i, 0, 0))
    return line.call(
        functools.partial(attend_back_kernel, masks, share),
        *dh, q, *kvs, w_out, *o, log, raw, cos, sin, q_gain,
        grid=(g, 2),
        in_specs=[chips(share, m)] * 2
        + [per_block((1, 1, HEAD, heads * b))]
        + [per_sequence((1, 2 * b, 2 * HEAD))] * len(kvs)
        + [
            pl.BlockSpec((width, m), lambda g, i, at: (at[2], 0)),
            half_rows,
            half_rows,
            per_block((1, 1, 1, heads * b)),
            per_block((1, 1, width, b)),
            table,
            table,
            constant((HEAD, 1)),
        ],
        out_specs=[half_rows, half_rows]
        + [per_sequence((1, 2 * b, 2 * HEAD))] * len(kvs)
        + [constant((HEAD, b))],
        scratch=[
            pltpu.VMEM((2 * HEAD, heads * b), BF),
            pltpu.VMEM((2 * HEAD, heads * b), BF),
            pltpu.VMEM((1, heads * b), F32),
            pltpu.VMEM((2 * HEAD, heads * b), F32),
            pltpu.VMEM((2 * b * len(kvs), 2 * HEAD), F32),
        ],
        out_shape=[shape_of((4, g, share, width))] * 2
        + [shape_of((g, 2 * b, 2 * HEAD))] * len(kvs)
        + [shape_of((HEAD, b), F32)],
        name="attend_back",
    )


def project_back_kernel(count, at_ref, *refs):
    dkv_refs = refs[:count]
    (
        dqa_ref, dqb_ref, raw_ref, xa_ref, xb_ref, wt_ref, cos_ref, sin_ref, kg_ref,
        dxb_ref, dxa_ref, dwa_ref, dwb_ref, dkg_ref, dag_ref,
    ) = refs[count:]

    @pl.when((pl.program_id(0) == 0) & (pl.program_id(1) == 0))
    def _():
        dkg_ref[...] = jnp.zeros_like(dkg_ref)
        dag_ref[...] = jnp.zeros_like(dag_ref)

    total = dkv_refs[0][0].astype(F32)
    for ref in dkv_refs[1:]:
        total += ref[0].astype(F32)
    t = total.T
    half = total.shape[0] // 2
    c, s = cos_ref[0], sin_ref[0]
    e1, e2 = t[:HALF], t[HALF:HEAD]
    e = jnp.concatenate([e1 * c + e2 * s, e2 * c - e1 * s], axis=0)
    v = raw_ref[0, 0]
    r = lax.rsqrt(jnp.mean(v * v, axis=0, keepdims=True) + EPS)
    unit = v * r
    ge = kg_ref[...] * e
    dk = r * (ge - unit * jnp.mean(ge * unit, axis=0, keepdims=True))
    dkg_ref[...] += e * unit
    dkv = jnp.concatenate([dk, t[HEAD:]], axis=0).T.astype(BF)
    width = dqa_ref.shape[3]
    gain_sum = jnp.zeros(dag_ref.shape, F32)
    for rows, dq_ref, x_ref, dx_ref, dw_ref in (
        (slice(0, half), dqa_ref, xa_ref, dxa_ref, dwa_ref),
        (slice(half, 2 * half), dqb_ref, xb_ref, dxb_ref, dwb_ref),
    ):
        dqkv = jnp.concatenate([join(dq_ref), dkv[rows]], axis=1)
        split(dw_ref, dqkv)
        dx = mm(dqkv, wt_ref[...])
        split(dx_ref, dx.astype(BF))
        gain_sum += jnp.sum(dx * join(x_ref).astype(F32), axis=0, keepdims=True)
    dag_ref[...] += gain_sum


def project_back(line, dkvs, dq, raw, xn, wt, cos, sin, k_gain):
    _, g, share, m = xn[0].shape
    b = 4 * share
    c = wt.shape[0]
    width = dq[0].shape[3]
    heads = width // HEAD
    table = pl.BlockSpec((1, HALF, b), lambda g, i, at: (i, 0, 0))
    return line.call(
        functools.partial(project_back_kernel, len(dkvs)),
        *dkvs, *dq, raw, *xn, wt, cos, sin, k_gain,
        grid=(g, 2),
        in_specs=[per_block((1, b, 2 * HEAD))] * len(dkvs)
        + [chips(share, width)] * 2
        + [pl.BlockSpec((1, 1, HEAD, b), lambda g, i, at: (g, i, heads, 0))]
        + [chips(share, m)] * 2
        + [constant((c, m)), table, table, constant((HEAD, 1))],
        out_specs=[chips(share, m)] * 2
        + [chips(share, c)] * 2
        + [constant((HEAD, b)), constant((1, m))],
        out_shape=[shape_of((4, g, share, m))] * 2
        + [shape_of((4, g, share, c))] * 2
        + [shape_of((HEAD, b), F32), shape_of((1, m), F32)],
        name="project_back",
    )


def ffn_kernel(
    tiles, at_ref, ha_ref, hb_ref, ga_ref, gb_ref, wg_ref, wu_ref, wd_ref, wgr_ref, wur_ref,
    db_ref, da_ref, act_ref, dgate_ref, dup_ref, keep_ref,
):
    t = pl.program_id(0)
    rows = ha_ref.shape[0]

    @pl.when(t < tiles)
    def _():
        for k, (h_ref, g_ref) in enumerate(((ha_ref, ga_ref), (hb_ref, gb_ref))):
            at = slice(k * rows, (k + 1) * rows)
            gate = mm(h_ref[...], wg_ref[...])
            up = mm(h_ref[...], wu_ref[...])
            dact = mm(g_ref[...], wd_ref[...], NT)
            sig = 1.0 / (1.0 + jnp.exp(-gate))
            silu = gate * sig
            act_ref[at, :] = (silu * up).astype(BF)
            dgate = (dact * up * (sig * (1.0 + gate * (1.0 - sig)))).astype(BF)
            dup = (dact * silu).astype(BF)
            dgate_ref[at, :] = dgate
            dup_ref[at, :] = dup
            keep_ref[t, 0, at, :] = dgate
            keep_ref[t, 1, at, :] = dup

    @pl.when(t >= tiles)
    def _():
        tile = keep_ref.shape[3]
        for k, d_ref in enumerate((da_ref, db_ref)):
            at = slice(k * rows, (k + 1) * rows)
            total = None
            for u in range(tiles):
                columns = slice(u * tile, (u + 1) * tile)
                part = mm(keep_ref[u, 0, at, :], wgr_ref[:, columns], NT)
                part += mm(keep_ref[u, 1, at, :], wur_ref[:, columns], NT)
                total = part if total is None else total + part
            d_ref[...] = total.astype(BF)


def ffn(line, hn, g, w_gate, w_up, w_down):
    r, m = hn[0].shape
    hidden = w_gate.shape[1] // 2
    tile, block = 256, 256
    tiles = hidden // tile

    def forward(t):
        return jnp.minimum(t, tiles - 1)

    def backward(t):
        return jnp.maximum(t - tiles, 0)

    columns = pl.BlockSpec((m, tile), lambda t, at: (0, at[2] * tiles + forward(t)))
    block_rows = pl.BlockSpec((block, hidden), lambda t, at: (backward(t), at[2]))
    d_block = pl.BlockSpec((r, block), lambda t, at: (0, backward(t)))
    hidden_block = pl.BlockSpec((2 * r, tile), lambda t, at: (0, forward(t)))
    return line.call(
        functools.partial(ffn_kernel, tiles), *hn, *g, w_gate, w_up, w_down, w_gate, w_up,
        grid=(tiles + m // block,),
        in_specs=[constant((r, m))] * 4
        + [
            columns,
            columns,
            pl.BlockSpec((tile, m), lambda t, at: (at[2] * tiles + forward(t), 0)),
            block_rows,
            block_rows,
        ],
        out_specs=[d_block, d_block, hidden_block, hidden_block, hidden_block],
        scratch=[pltpu.VMEM((tiles, 2, 2 * r, tile), BF)],
        out_shape=[shape_of((r, m))] * 2 + [shape_of((2 * r, hidden))] * 3,
        name="ffn",
        limit=52 * MIB,
    )


def down_kernel(at_ref, act_ref, wd_ref, b_ref, a_ref):
    r = a_ref.shape[0]
    y = mm(act_ref[...], wd_ref[...]).astype(BF)
    a_ref[...] = y[:r]
    b_ref[...] = y[r:]


def down(line, act, w_down):
    rows, hidden = act.shape
    m = w_down.shape[1]
    block = 256
    out = pl.BlockSpec((rows // 2, block), lambda t, at: (0, t))
    return line.call(
        down_kernel, act, w_down,
        grid=(m // block,),
        in_specs=[
            constant((rows, hidden)),
            pl.BlockSpec((hidden, block), lambda t, at: (at[2], t)),
        ],
        out_specs=[out, out],
        out_shape=[shape_of((rows // 2, m))] * 2,
        name="down",
    )


def chip_sum_kernel(at_ref, a_ref, b_ref, out_ref):
    rows = out_ref.shape[0]
    for k in range(0, rows, rows // 8):
        at = slice(k, k + rows // 8)
        out_ref[at] = (a_ref[at].astype(F32) + b_ref[at].astype(F32)).astype(BF)


def chip_sum(line, a, b):
    return line.small(chip_sum_kernel, a, b, out_shape=shape_of(a.shape), name="chip_sum")


def write_four(ref, g, value):
    for k in range(4):
        ref[k, g] = value


def sum_four(ref, g):
    total = ref[0, g].astype(F32)
    for k in range(1, 4):
        total += ref[k, g].astype(F32)
    return total


def mask_kernel(n_rows, at_ref, g_ref, out_ref):
    seqs, share, _ = g_ref.shape
    first = at_ref[0] * n_rows + at_ref[1] * share
    p = first + lax.broadcasted_iota(jnp.int32, (share, 1), 0)
    for g in range(seqs):
        write_four(out_ref, g, jnp.where(p < at_ref[3 + g], g_ref[g].astype(F32), 0.0).astype(BF))


def mask(line, grad, b):
    g, share, m = grad.shape
    return line.small(
        functools.partial(mask_kernel, b), grad, out_shape=shape_of((4, g, share, m)), name="mask"
    )


def middle_kernel(at_ref, parts_ref, tok_ref, gain_ref, hn_ref, h_ref):
    for g in range(tok_ref.shape[0]):
        h = tok_ref[g].astype(F32) + sum_four(parts_ref, g)
        h_ref[g] = h
        r = lax.rsqrt(jnp.mean(h * h, axis=-1, keepdims=True) + EPS)
        write_four(hn_ref, g, (h * r * gain_ref[...]).astype(BF))


def middle(line, parts, tok, gain):
    return line.small(
        middle_kernel, parts, tok, gain,
        out_shape=[shape_of(parts.shape), shape_of(tok.shape, F32)], name="middle",
    )


def middle_back_kernel(at_ref, parts_ref, h_ref, g_ref, gain_ref, low_ref, dh_ref, dg_ref):
    dg = jnp.zeros(dg_ref.shape, F32)
    for g in range(h_ref.shape[0]):
        e = sum_four(parts_ref, g)
        h = h_ref[g]
        r = lax.rsqrt(jnp.mean(h * h, axis=-1, keepdims=True) + EPS)
        unit = h * r
        ge = gain_ref[...] * e
        dh = g_ref[g].astype(F32) + r * (ge - unit * jnp.mean(ge * unit, axis=-1, keepdims=True))
        dh_ref[g] = dh
        write_four(low_ref, g, dh.astype(BF))
        dg += jnp.sum(e * unit, axis=0, keepdims=True)
    dg_ref[...] = dg


def middle_back(line, parts, h, grad, gain):
    return line.small(
        middle_back_kernel, parts, h, grad[0], gain,
        out_shape=[shape_of(parts.shape), shape_of(h.shape, F32), shape_of(gain.shape, F32)],
        name="middle_back",
    )


def finish_mixed_kernel(at_ref, parts_ref, h_ref, out_ref):
    for g in range(h_ref.shape[0]):
        out_ref[g] = (h_ref[g] + sum_four(parts_ref, g)).astype(BF)


def finish_mixed(line, parts, h):
    return line.small(
        finish_mixed_kernel, parts, h, out_shape=shape_of(h.shape), name="finish_mixed"
    )


def finish_tokens_kernel(at_ref, parts_ref, tok_ref, dh_ref, gain_ref, out_ref):
    for g in range(tok_ref.shape[0]):
        e = sum_four(parts_ref, g)
        v = tok_ref[g].astype(F32)
        r = lax.rsqrt(jnp.mean(v * v, axis=-1, keepdims=True) + EPS)
        unit = v * r
        ge = gain_ref[...] * e
        out_ref[g] = dh_ref[g] + r * (ge - unit * jnp.mean(ge * unit, axis=-1, keepdims=True))


def finish_tokens(line, parts, tok, dh, gain):
    return line.small(
        finish_tokens_kernel, parts, tok, dh, gain, out_shape=shape_of(dh.shape, F32), name="finish_tokens"
    )


def turn_kernel(at_ref, a_ref, b_ref, out_ref):
    rows = a_ref.shape[0]
    out_ref[:, :rows] = a_ref[...].astype(F32).T.astype(BF)
    out_ref[:, rows:] = b_ref[...].astype(F32).T.astype(BF)


def turn(line, pair):
    r, m = pair[0].shape
    block = 512
    columns = pl.BlockSpec((r, block), lambda k, at: (0, k))
    return line.call(
        turn_kernel, *pair,
        grid=(m // block,),
        in_specs=[columns, columns],
        out_specs=pl.BlockSpec((block, 2 * r), lambda k, at: (k, 0)),
        out_shape=shape_of((m, 2 * r)),
        name="turn",
    )


def both_rows(left_ref, ra_ref, rb_ref, at=slice(None)):
    rows = ra_ref.shape[0]
    return mm(left_ref[:, :rows], ra_ref[:, at]) + mm(left_ref[:, rows:], rb_ref[:, at])


def grad_kernel(start, begins, at_ref, left_ref, ra_ref, rb_ref, *refs):
    out_ref, acc_ref = refs[-2:]
    width = out_ref.shape[1]
    acc_ref[...] = both_rows(left_ref, ra_ref, rb_ref, slice(start, start + width))
    for begin, ref in zip(begins, refs):
        low, high = max(begin, start), min(begin + ref.shape[1], start + width)
        acc_ref[:, low - start : high - start] += ref[:, low - begin : high - begin].astype(F32)
    out_ref[...] = acc_ref[...].astype(BF)


def grad_whole_kernel(starts, final, at_ref, left_ref, ra_ref, rb_ref, *refs):
    out_ref, acc_ref = refs[-2:]

    def own():
        acc_ref[...] = both_rows(left_ref, ra_ref, rb_ref)
        for start, ref in zip(starts, refs):
            acc_ref[:, start : start + ref.shape[1]] += ref[...].astype(F32)
        out_ref[...] = acc_ref[...].astype(out_ref.dtype)

    if final:
        pl.when(pl.program_id(0) == 0)(own)

        @pl.when(pl.program_id(0) == 1)
        def _():
            out_ref[...] = refs[-3][...].astype(F32)
    else:
        own()


class WeightGrad:
    def __init__(self, line, left, right):
        self.line, self.left, self.right = line, left, right
        self.count = count = lax.axis_size("narrow")
        m, rows = left.shape
        self.r = rows // 2
        self.c = right[0][0].shape[1]
        self.block = m // count
        far = [bit for k in range(1, count.bit_length()) if (bit := count >> k) > TP_BIT]
        self.orders = {True: [1] + far, False: far + [1]}
        self.received = []

    def call(self, kernel, masks, extra, **kwargs):
        step = masks[1] - masks[0] if len(masks) > 1 else 0
        assert masks == [masks[0] + k * step for k in range(len(masks))]
        fixed = len(masks) == 1

        def which(k):
            return 0 if fixed else k

        arrays = [self.left, self.right[0][0], self.right[1][0]]
        specs = [
            pl.BlockSpec(
                (self.block, 2 * self.r), lambda k, at: (at[0] ^ (masks[0] + which(k) * step), 0)
            )
        ] + [pl.BlockSpec((self.r, self.c), lambda k, at, rows=rows: (rows, 0)) for _, rows in self.right]
        for array, begin, stride in extra:
            arrays.append(array)
            specs.append(
                pl.BlockSpec(
                    (None, self.block, array.shape[2]),
                    lambda k, at, begin=begin, stride=stride: (begin + which(k) * stride, 0, 0),
                )
            )
        return self.line.call(kernel, *arrays, in_specs=specs, name="grad", **kwargs)

    def send(self, stage, start=0, width=None, near_first=True):
        width = width or self.c
        order = self.orders[near_first]
        bit = order[stage]
        away = [k for k in range(self.count) if k & bit and not any(k & b for b in order[:stage])]
        extra, begins = [], []
        for masks, begin, size, array in self.received:
            if away[0] in masks and begin < start + width and start < begin + size:
                stride = masks.index(away[1]) - masks.index(away[0]) if len(away) > 1 else 0
                extra.append((array, masks.index(away[0]), stride))
                begins.append(begin)
        part = self.call(
            functools.partial(grad_kernel, start, begins), away, extra,
            grid=(len(away),),
            out_specs=pl.BlockSpec((None, self.block, width), lambda k, at: (k, 0, 0)),
            out_shape=shape_of((len(away), self.block, width)),
            scratch=[pltpu.VMEM((self.block, width), F32)],
        )
        got = swap(part, bit, 0)
        self.received.append(([k ^ bit for k in away], start, width, got))
        return got

    def rest(self, start=0, width=None):
        for stage in range(1, len(self.orders[True])):
            got = self.send(stage, start, width)
        return got

    def far(self, start=0, width=None):
        for stage in range(len(self.orders[False]) - 1):
            got = self.send(stage, start, width, False)
        return got

    def near(self, start=0, width=None):
        return self.send(len(self.orders[False]) - 1, start, width, False)

    def whole(self, mask, final, **kwargs):
        extra = [
            (array, masks.index(mask), 0)
            for masks, _, _, array in self.received
            if mask in masks
        ]
        starts = [begin for masks, begin, _, _ in self.received if mask in masks]
        if final:
            extra.append((self.peer, 0, 0))
        return self.call(
            functools.partial(grad_whole_kernel, starts, final), [mask], extra,
            scratch=[pltpu.VMEM((self.block, self.c), F32)], **kwargs,
        )

    def last(self):
        part = self.whole(
            TP_BIT, False,
            grid=(1,),
            out_specs=pl.BlockSpec((None, self.block, self.c), lambda k, at: (0, 0, 0)),
            out_shape=shape_of((1, self.block, self.c)),
        )
        self.peer = swap(part, TP_BIT, 0)

    def finish(self):
        return self.whole(
            0, True,
            grid=(2,),
            out_specs=pl.BlockSpec((self.block, self.c), lambda k, at: (0, k ^ at[2])),
            out_shape=shape_of((self.block, 2 * self.c), F32),
        )


def prepare_kernel(at_ref, q_ref, k_ref, v_ref, out_ref):
    width = k_ref.shape[1] // 2

    def own(ref):
        x = ref[...].astype(F32)
        return jnp.where(at_ref[2] == 0, x[:, :width], x[:, width:])

    x = jnp.concatenate([q_ref[...].astype(F32), own(k_ref), own(v_ref)], axis=1)
    out_ref[...] = x.T.astype(BF)


def prepare(line, w_query, w_key, w_value):
    m = w_query.shape[0]
    width, kv_width = w_query.shape[1] // 2, w_key.shape[1]
    rows = 512
    kv = pl.BlockSpec((rows, kv_width), lambda j, at: (j, 0))
    return line.call(
        prepare_kernel, w_query, w_key, w_value,
        grid=(m // rows,),
        in_specs=[pl.BlockSpec((rows, width), lambda j, at: (j, at[2])), kv, kv],
        out_specs=pl.BlockSpec((width + kv_width, rows), lambda j, at: (0, j)),
        out_shape=shape_of((width + kv_width, m)),
        name="prepare",
    )


def swap(x, narrow_mask, wide_mask):
    wide = lax.axis_size("wide")
    count = lax.axis_size("narrow") * wide
    mask = narrow_mask * wide + wide_mask
    return lax.ppermute(x, AXES, [(d, d ^ mask) for d in range(count)])


def chip_groups():
    wide = lax.axis_size("wide")
    count = lax.axis_size("narrow") * wide
    masks = (0, 2, TP_BIT * wide, TP_BIT * wide + 2)
    groups = sorted({tuple(sorted(d ^ mask for mask in masks)) for d in range(count)})
    return [list(group) for group in groups]


def exchange(x):
    return lax.all_to_all(x, AXES, 0, 0, tiled=True, axis_index_groups=chip_groups())


def gathered(x):
    a = exchange(x)
    return a, swap(a, 0, 1)


def scatter(line, a, b, shape):
    return exchange(chip_sum(line, a, b).reshape(shape))


def row_masks(count):
    return [(k & 1) | ((k >> 1) << 2) for k in range(count // 2)]


class Total:
    def __init__(self, x):
        self.x = x
        narrow = [1 << k for k in range(lax.axis_size("narrow").bit_length() - 1)]
        wide = [1 << k for k in range(lax.axis_size("wide").bit_length() - 1)]
        self.steps = [(0, k) for k in wide] + [(TP_BIT, 0)] + [(k, 0) for k in narrow if k != TP_BIT]

    def step(self, line):
        sent = swap(after(self.x, line.last[0]), *self.steps.pop(0))
        self.x = self.x + sent
        return sent

    def rest(self, line):
        while self.steps:
            self.step(line)
        return self.x


def after(x, *others):
    return lax.optimization_barrier((x, *others))[0]


def unit_rows(v):
    r = lax.rsqrt(jnp.mean(v * v, axis=-1, keepdims=True) + EPS)
    return v * r, r


def shards(
    tokens, lengths, attn_gain, w_query, key_matrix, value_matrix, q_gain, k_gain, w_out, ffn_gain,
    w_gate, w_up, w_down, out_grad,
):
    n, w = lax.axis_index("narrow"), lax.axis_index("wide")
    count = lax.axis_size("narrow")
    share, seqs, m = tokens.shape
    b = share * lax.axis_size("wide")
    half = (n // TP_BIT) % 2

    inside = position_inside(jnp.arange(b, dtype=jnp.int32), share, w)
    positions = jnp.stack([block_of(n, 0, i) * b + inside for i in range(2)]).astype(F32)
    freqs = jnp.exp(-math.log(10000.0) * jnp.arange(HALF, dtype=F32) * 2.0 / HEAD)
    angles = positions[:, None, :] * freqs[None, :, None]
    cos, sin = jnp.cos(angles), jnp.sin(angles)
    qg, kg = q_gain[:, None], k_gain[:, None]
    line = Line(jnp.concatenate([jnp.stack([n, w, half]).astype(jnp.int32), lengths]))
    masks = row_masks(count)
    rows = seqs * b
    shape = (4, seqs, share, m)

    def flat(pair):
        return tuple(x.reshape(rows, x.shape[-1]) for x in pair)

    def whole(pair):
        return tuple((x, 0) for x in flat(pair))

    def halves(x):
        return ((x, 0), (x, 1))

    tok = jnp.moveaxis(tokens, 1, 0)
    out_grad = jnp.moveaxis(out_grad, 1, 0)

    unit, _ = unit_rows(tok.astype(F32))
    sent = exchange(jnp.broadcast_to((unit * attn_gain).astype(BF)[None], shape))
    grad = mask(line, out_grad, b)
    wt = prepare(line, w_query, key_matrix, value_matrix)
    sent = after(sent, wt)
    xn = (sent, swap(sent, 0, 1))
    g_own = exchange(after(grad, sent))
    kv, q, raw = project(line, xn, wt, cos, sin, qg, kg)
    kvs = [swap(kv, k, 0) if k else kv for k in masks]
    xn_turned = turn(line, flat(xn))
    line.wait(g_own)
    pb, pa, oa, ob, log = attend(line, q, kvs, masks, w_out, share)
    pb = swap(pb, 0, 1)
    g_all = (g_own, swap(g_own, 0, 1))
    parts = scatter(line, *flat((pa, pb)), shape)
    g_turned = turn(line, flat(g_all))
    hn, h = middle(line, parts, tok, ffn_gain[None])
    hn = gathered(hn)

    db, da, act, dgate, dup = ffn(line, flat(hn), flat(g_all), w_gate, w_up, w_down)
    db = swap(db, 0, 1)
    c = act.shape[1]
    first, rest = (0, c // 4), (c // 4, 3 * c // 4)
    early, late = (0, 3 * c // 8), (3 * c // 8, 5 * c // 8)
    d_down = WeightGrad(line, g_turned, halves(act))
    d_down.send(0)
    parts = scatter(line, da, db, shape)
    hn_turned = turn(line, flat(hn))
    d_gate = WeightGrad(line, hn_turned, halves(dgate))
    d_up = WeightGrad(line, hn_turned, halves(dup))
    u_first = d_up.far(*early)
    g_first = d_gate.send(0, *first)
    g_rest = d_gate.send(0, *rest)
    dhl, dh, ffn_gain_grad = middle_back(line, parts, h, grad, ffn_gain[None])
    dhl = exchange(dhl)
    line.wait(u_first)
    d_first = d_down.rest(*first)
    yb, ya = down(line, act, w_down)
    yb = swap(yb, 0, 1)
    d_rest = d_down.rest(*rest)
    dhl = after(dhl, line.last[0], g_first, d_first, yb)
    dhl = (dhl, swap(dhl, 0, 1))
    mixed_parts = scatter(line, ya, yb, shape)

    back = attend_back(line, dhl, q, kvs, masks, w_out, (oa, ob), log, raw, cos, sin, qg, share)
    dq, dkvs, dqg = back[:2], after(tuple(back[2:-1]), g_rest, d_rest), back[-1]
    dkvs = [swap(x, k, 0) if k else x for x, k in zip(dkvs, masks)]
    dhl_turned = turn(line, flat(dhl))
    dxb, dxa, dwa, dwb, dkg, dag = project_back(line, dkvs, dq, raw, xn, wt, cos, sin, kg)
    dxb = swap(dxb, 0, 1)
    mixed = finish_mixed(line, mixed_parts, h)
    parts = scatter(line, *flat((dxa, dxb)), shape)
    g_z = d_gate.rest()
    d_up.send(0, *late)
    d_qkv = WeightGrad(line, xn_turned, whole((dwa, dwb)))
    d_qkv.send(0)
    d_out = WeightGrad(line, dhl_turned, whole((oa, ob)))
    d_out.send(0)
    d_up.near(*early)
    gains = jnp.concatenate(
        [dag[0] / attn_gain, ffn_gain_grad[0], jnp.sum(dqg, axis=1), jnp.sum(dkg, axis=1)]
    )
    gains = Total(gains.reshape(-1, 128))
    sent = gains.step(line)
    d_down.last()
    line.wait(g_z, sent)
    d_tokens = finish_tokens(line, parts, tok, dh, attn_gain[None])
    sent = gains.step(line)
    d_qkv.rest()
    d_out.rest()
    u_z = d_up.rest(*late)
    d_gate.last()
    down_grad = d_down.finish()
    line.wait(sent)
    d_qkv.last()
    sent = gains.step(line)
    gate_grad = d_gate.finish()
    line.wait(u_z)
    d_up.last()
    d_out.last()
    line.wait(sent)
    qkv_grad = d_qkv.finish()
    sent = gains.step(line)
    out_grad_t = d_out.finish()
    line.wait(sent)
    up_grad = d_up.finish()
    gains = gains.rest(line).reshape(-1)
    width = dq[0].shape[3]
    columns = dwa.shape[3]
    qkv_grad = qkv_grad.reshape(-1, 2, columns)
    query_grad = qkv_grad[:, :, :width].reshape(-1, 2 * width)
    return (
        jnp.moveaxis(mixed, 0, 1),
        jnp.moveaxis(d_tokens, 0, 1),
        gains[:m],
        query_grad,
        qkv_grad[:, :, width : width + HEAD].reshape(-1, 2 * HEAD),
        qkv_grad[:, :, width + HEAD :].reshape(-1, 2 * HEAD),
        gains[2 * m : 2 * m + HEAD],
        gains[2 * m + HEAD :],
        out_grad_t,
        gains[m : 2 * m],
        gate_grad,
        up_grad,
        down_grad,
    )


def solution(mesh):
    rows = P(AXES, None, None)
    columns = P(None, "wide")
    block = P("narrow", "wide")
    in_specs = (
        rows, P(), P(), columns, columns, columns, P(), P(), P("wide", None), P(), columns, columns,
        P("wide", None), rows,
    )
    out_specs = (
        rows, rows, P(), block, block, block, P(), P(), block, P(), block, block, block,
    )
    return jax.shard_map(shards, mesh=mesh, in_specs=in_specs, out_specs=out_specs, check_vma=False)
```

profile of v0, /device:TPU:0, one launch (start us, length us, event | category | flops | bytes accessed | tf_op | source)
XLA Modules:
  0.0 536.7 jit_solution(8274030173939859434)
XLA Ops:
  4.8 5.4 all-to-all-start
  12.5 4.7 prepare.1.refs_0_.refs_3_.refs_10_
  17.2 17.9 %all-to-all-done.refs_1_.refs_8_ = bf16[4,2,64,2048]{3,2,1,0:T(8,128)(2,1)S(1)} async-done(((bf16[4,2,64,2048]{3,2,1,0:T(8,128)(2,1)}), bf16[4,2,64,2048]{3,2,1,0:T(8,128)(2,1)S(1)}, u32[]{:S(2)}, u32[]{:S(2)}) %all-to-all-start) | async-done | bytes 2097184 | tf_op jit(solution)/shard_map/all_to_all | solution.py:823
  36.4 3.6 all-to-all-start.1
  40.6 3.9 collective-permute-done.refs_2_.refs_9_
  44.6 6.5 %project.1 = (bf16[2,512,128]{2,1,0:T(8,128)(2,1)S(1)}, bf16[2,2,64,1024]{3,2,1,0:T(8,128)(2,1)S(1)}, f32[2,2,320,256]{3,2,1,0:T(8,128)}) custom-call(s32[5]{0:T(128)S(1)} %pad_add_fusion.at_ref, bf16[384,2048]{1,0:T(8,128)(2,1)} %prepare.1.refs_0_.refs_3_.refs_10_, bf16[4,2,64,2048]{3,2,1,0:T(8,128)(2,1)} %copy-done.63, ...), custom_call_target="tpu_custom_call" | custom-call | flops 5000000000 | tf_op jit(solution)/shard_map/project/pallas_call | solution.py:50
  51.8 3.6 collective-permute-start.3
  56.2 5.8 %turn.4.refs_0_.refs_1_.refs_2_ = bf16[2048,1024]{1,0:T(8,128)(2,1)} custom-call(s32[5]{0:T(128)S(1)} %pad_add_fusion.at_ref, bf16[2,512,128]{2,1,0:T(8,128)(2,1)S(1)} %get-tuple-element.59.refs_0_.refs_3_.refs_4_, bf16[512,2048]{1,0:T(8,128)(2,1)} %bitcast.93, bf16[512,2048]{1,0:T(8,128)(2,1)} %bitcast.8.refs_2_), custom_call_target="tpu_custom_call" | custom-call | flops 5000000000 | tf_op jit(solution)/shard_map/turn/pallas_call | solution.py:50
  62.0 7.5 %collective-permute-done.3.refs_6_.refs_7_ = bf16[2,512,128]{2,1,0:T(8,128)(2,1)S(1)} collective-permute-done((bf16[2,512,128]{2,1,0:T(8,128)(2,1)S(1)}, bf16[2,512,128]{2,1,0:T(8,128)(2,1)S(1)}, u32[]{:S(2)}, u32[]{:S(2)}) %collective-permute-start.3) | collective-permute-done | bytes 262176 | tf_op jit(solution)/shard_map/ppermute | solution.py:811
  69.5 9.6 %collective-permute-done.2.refs_5_.refs_6_ = bf16[2,512,128]{2,1,0:T(8,128)(2,1)S(1)} collective-permute-done((bf16[2,512,128]{2,1,0:T(8,128)(2,1)S(1)}, bf16[2,512,128]{2,1,0:T(8,128)(2,1)S(1)}, u32[]{:S(2)}, u32[]{:S(2)}) %collective-permute-start.2) | collective-permute-done | bytes 262176 | tf_op jit(solution)/shard_map/ppermute | solution.py:811
  80.4 9.4 %attend.1 = (bf16[4,2,64,2048]{3,2,1,0:T(8,128)(2,1)}, bf16[4,2,64,2048]{3,2,1,0:T(8,128)(2,1)}, bf16[4,2,64,256]{3,2,1,0:T(8,128)(2,1)S(1)}, bf16[4,2,64,256]{3,2,1,0:T(8,128)(2,1)S(1)}, f32[2,2,1,1024]{3,2,1,0:T(1,128)S(1)}) custom-call(s32[5]{0:T(128)S(1)} %pad_add_fusion.at_ref, bf16[2048,1024]{1,0:T(8,128)(2,1)} %turn.4.refs_0_.refs_1_.refs_2_, ...), custom_call_target="tpu_custom_call" | custom-call | flops 5000000000 | tf_op jit(solution)/shard_map/attend/pallas_call | solution.py:50
  90.0 4.4 collective-permute-done.4
  99.9 3.7 all-to-all-start.2
  104.1 4.1 collective-permute-done.5
  109.5 5.8 %turn.5.refs_0_.refs_1_.refs_2_ = bf16[2048,1024]{1,0:T(8,128)(2,1)} custom-call(s32[5]{0:T(128)S(1)} %pad_add_fusion.at_ref, bf16[512,2048]{1,0:T(8,128)(2,1)} %copy-done.5, bf16[512,2048]{1,0:T(8,128)(2,1)} %bitcast.89, bf16[512,2048]{1,0:T(8,128)(2,1)} %bitcast.97), custom_call_target="tpu_custom_call" | custom-call | flops 5000000000 | tf_op jit(solution)/shard_map/turn/pallas_call | solution.py:50
  115.3 14.0 %all-to-all-done.2.refs_1_ = bf16[4,2,64,2048]{3,2,1,0:T(8,128)(2,1)S(1)} async-done(((bf16[4,2,64,2048]{3,2,1,0:T(8,128)(2,1)}), bf16[4,2,64,2048]{3,2,1,0:T(8,128)(2,1)S(1)}, u32[]{:S(2)}, u32[]{:S(2)}) %all-to-all-start.2) | async-done | bytes 2097184 | tf_op jit(solution)/shard_map/all_to_all | solution.py:823
  132.6 28.0 %all_to_all.40 = bf16[4,2,64,2048]{3,2,1,0:T(8,128)(2,1)S(1)} all-to-all(bf16[4,2,64,2048]{3,2,1,0:T(8,128)(2,1)S(1)} %get-tuple-element.64.refs_0_), channel_id=1, replica_groups={{0,2,8,10},{1,3,9,11},{4,6,12,14},{5,7,13,15},{16,18,24,26},{17,19,25,2..., dimensions={0} | all-to-all | bytes 4194304 | tf_op jit(solution)/shard_map/all_to_all | solution.py:823
  160.7 4.1 collective-permute-done.6
  166.2 32.7 %ffn.1 = (bf16[512,2048]{1,0:T(8,128)(2,1)}, bf16[512,2048]{1,0:T(8,128)(2,1)}, bf16[1024,1024]{1,0:T(8,128)(2,1)}, bf16[1024,1024]{1,0:T(8,128)(2,1)}, bf16[1024,1024]{1,0:T(8,128)(2,1)}) custom-call(s32[5]{0:T(128)S(1)} %pad_add_fusion.at_ref, bf16[4,2,64,2048]{3,2,1,0:T(8,128)(2,1)} %copy-done, bf16[512,2048]{1,0:T(8,128)(2,1)} %bitcast.91, ...), custom_call_target="tpu_custom_call" | custom-call | flops 5000000000 | tf_op jit(solution)/shard_map/ffn/pallas_call | solution.py:50
  199.0 6.6 %grad.24.refs_0_ = bf16[4,256,1024]{2,1,0:T(8,128)(2,1)} custom-call(s32[5]{0:T(128)S(1)} %pad_add_fusion.at_ref, bf16[512,2048]{1,0:T(8,128)(2,1)} %get-tuple-element.65.refs_0_, bf16[2048,1024]{1,0:T(8,128)(2,1)} %turn.5.refs_0_.refs_1_.refs_2_, bf16[1024,1024]{1,0:T(8,128)(2,1)} %get-tuple-element.66.refs_2_.refs_3_.refs_4_.refs_1_, ...), custom_call_target="tpu_custom_call" | custom-call | flops 5000000000 | tf_op jit(solution)/shard_map/grad/pallas_call | solution.py:50
  209.6 3.6 all-to-all-start.4
  216.6 5.9 %turn.6.refs_0_.refs_1_.refs_2_ = bf16[2048,1024]{1,0:T(8,128)(2,1)} custom-call(s32[5]{0:T(128)S(1)} %pad_add_fusion.at_ref, bf16[512,2048]{1,0:T(8,128)(2,1)} %copy-done.4, bf16[512,2048]{1,0:T(8,128)(2,1)} %bitcast.92, bf16[512,2048]{1,0:T(8,128)(2,1)} %bitcast.96), custom_call_target="tpu_custom_call" | custom-call | flops 5000000000 | tf_op jit(solution)/shard_map/turn/pallas_call | solution.py:50
  222.4 5.6 %grad.25.refs_0_ = bf16[4,256,384]{2,1,0:T(8,128)(2,1)} custom-call(s32[5]{0:T(128)S(1)} %pad_add_fusion.at_ref, bf16[2048,1024]{1,0:T(8,128)(2,1)} %turn.6.refs_0_.refs_1_.refs_2_, bf16[2048,1024]{1,0:T(8,128)(2,1)} %turn.6.refs_0_.refs_1_.refs_2_, bf16[1024,1024]{1,0:T(8,128)(2,1)} %get-tuple-element.68.refs_2_.refs_3_.refs_4_, ...), custom_call_target="tpu_custom_call" | custom-call | flops 5000000000 | tf_op jit(solution)/shard_map/grad/pallas_call | solution.py:50
  228.0 6.7 %collective-permute-start.8 = (bf16[4,256,384]{2,1,0:T(8,128)(2,1)}, bf16[4,256,384]{2,1,0:T(8,128)(2,1)}, u32[]{:S(2)}, u32[]{:S(2)}) collective-permute-start(bf16[4,256,384]{2,1,0:T(8,128)(2,1)} %grad.25.refs_0_), channel_id=1, source_target_pairs={{0,16},{1,17},{2,18},{3,19},{4,20},{5,21},{6,22},{7,23},{8,24},{9,... | collective-permute-start | bytes 2359304 | tf_op jit(solution)/shard_map/ppermute | solution.py:811
  234.7 4.3 grad.26.refs_0_
  239.0 6.0 %grad.27.refs_0_ = bf16[4,256,768]{2,1,0:T(8,128)(2,1)} custom-call(s32[5]{0:T(128)S(1)} %pad_add_fusion.at_ref, bf16[4,256,256]{2,1,0:T(8,128)(2,1)S(1)} %grad.26.refs_0_, bf16[2048,1024]{1,0:T(8,128)(2,1)} %turn.6.refs_0_.refs_1_.refs_2_, bf16[1024,1024]{1,0:T(8,128)(2,1)} %get-tuple-element.69.refs_2_.refs_3_, ...), custom_call_target="tpu_custom_call" | custom-call | flops 5000000000 | tf_op jit(solution)/shard_map/grad/pallas_call | solution.py:50
  245.8 3.0 all-to-all-done.4.refs_1_
  251.5 2.9 middle_back.1
  255.3 4.5 all-to-all-start.5
  259.8 3.2 collective-permute-done.9.refs_5_.refs_4_
  263.0 6.7 %collective-permute-done.8.refs_1_.refs_4_.refs_5_ = bf16[4,256,384]{2,1,0:T(8,128)(2,1)} collective-permute-done((bf16[4,256,384]{2,1,0:T(8,128)(2,1)}, bf16[4,256,384]{2,1,0:T(8,128)(2,1)}, u32[]{:S(2)}, u32[]{:S(2)}) %collective-permute-start.8) | collective-permute-done | bytes 786464 | tf_op jit(solution)/shard_map/ppermute | solution.py:811
  269.7 3.1 grad.28.refs_0_
  272.9 10.2 %down.1 = (bf16[512,2048]{1,0:T(8,128)(2,1)}, bf16[512,2048]{1,0:T(8,128)(2,1)}) custom-call(s32[5]{0:T(128)S(1)} %pad_add_fusion.at_ref, bf16[2,256,256]{2,1,0:T(8,128)(2,1)S(1)} %grad.28.refs_0_, bf16[1024,1024]{1,0:T(8,128)(2,1)} %get-tuple-element.66.refs_2_.refs_3_.refs_4_.refs_1_, bf16[2048,2048]{1,0:T(8,128)(2,1)} %refs_2_.3), custom_call_target="tpu_custom_call" | custom-call | flops 5000000000 | tf_op jit(solution)/shard_map/down/pallas_call | solution.py:50
  284.8 3.6 grad.29.refs_0_
  289.3 8.1 %collective-permute-done.11.refs_4_ = bf16[4,256,256]{2,1,0:T(8,128)(2,1)S(1)} collective-permute-done((bf16[4,256,256]{2,1,0:T(8,128)(2,1)S(1)}, bf16[4,256,256]{2,1,0:T(8,128)(2,1)S(1)}, u32[]{:S(2)}, u32[]{:S(2)}) %collective-permute-start.11) | collective-permute-done | bytes 524320 | tf_op jit(solution)/shard_map/ppermute | solution.py:811
  306.0 4.5 all-to-all-start.6
  310.5 14.7 %attend_back.1 = (bf16[4,2,64,256]{3,2,1,0:T(8,128)(2,1)S(1)}, bf16[4,2,64,256]{3,2,1,0:T(8,128)(2,1)S(1)}, bf16[2,512,128]{2,1,0:T(8,128)(2,1)S(1)}, bf16[2,512...) custom-call(s32[5]{0:T(128)S(1)} %pad_add_fusion.at_ref, ...), custom_call_target="tpu_custom_call" | custom-call | flops 5000000000 | tf_op jit(solution)/shard_map/attend_back/pallas_call | solution.py:50
  325.2 11.3 %collective-permute-done.14.refs_5_ = bf16[4,256,768]{2,1,0:T(8,128)(2,1)} collective-permute-done((bf16[4,256,768]{2,1,0:T(8,128)(2,1)}, bf16[4,256,768]{2,1,0:T(8,128)(2,1)}, u32[]{:S(2)}, u32[]{:S(2)}) %collective-permute-start.14) | collective-permute-done | bytes 1572896 | tf_op jit(solution)/shard_map/ppermute | solution.py:811
  339.2 3.0 collective-permute-start.18
  342.2 5.9 %turn.7.refs_0_.refs_1_ = bf16[2048,1024]{1,0:T(8,128)(2,1)} custom-call(s32[5]{0:T(128)S(1)} %pad_add_fusion.at_ref, bf16[4,2,64,256]{3,2,1,0:T(8,128)(2,1)S(1)} %get-tuple-element.79.refs_0_.refs_5_, bf16[512,2048]{1,0:T(8,128)(2,1)} %bitcast.19.refs_1_, bf16[512,2048]{1,0:T(8,128)(2,1)} %bitcast.20.refs_2_), custom_call_target="tpu_custom_call" | custom-call | flops 5000000000 | tf_op jit(solution)/shard_map/turn/pallas_call | solution.py:50
  348.0 12.1 %collective-permute-done.17.refs_3_ = bf16[2,512,128]{2,1,0:T(8,128)(2,1)S(1)} collective-permute-done((bf16[2,512,128]{2,1,0:T(8,128)(2,1)S(1)}, bf16[2,512,128]{2,1,0:T(8,128)(2,1)S(1)}, u32[]{:S(2)}, u32[]{:S(2)}) %collective-permute-start.17) | collective-permute-done | bytes 262176 | tf_op jit(solution)/shard_map/ppermute | solution.py:811
  360.1 4.8 collective-permute-done.18.refs_4_
  365.0 7.9 %project_back.1 = (bf16[4,2,64,2048]{3,2,1,0:T(8,128)(2,1)}, bf16[4,2,64,2048]{3,2,1,0:T(8,128)(2,1)}, bf16[4,2,64,384]{3,2,1,0:T(8,128)(2,1)}, bf16[4,2,64,384]...) custom-call(s32[5]{0:T(128)S(1)} %pad_add_fusion.at_ref, bf16[2048,1024]{1,0:T(8,128)(2,1)} %turn.7.refs_0_.refs_1_, ...), custom_call_target="tpu_custom_call" | custom-call | flops 5000000000 | tf_op jit(solution)/shard_map/project_back/pallas_call | solution.py:50
  381.3 3.7 all-to-all-start.7
  386.4 3.9 grad.30.refs_0_
  391.7 6.0 %grad.31.refs_0_ = bf16[4,256,640]{2,1,0:T(8,128)(2,1)} custom-call(s32[5]{0:T(128)S(1)} %pad_add_fusion.at_ref, bf16[2,256,1024]{2,1,0:T(8,128)(2,1)S(1)} %grad.30.refs_0_, bf16[2048,1024]{1,0:T(8,128)(2,1)} %turn.6.refs_0_.refs_1_.refs_2_, bf16[1024,1024]{1,0:T(8,128)(2,1)} %get-tuple-element.68.refs_2_.refs_3_.refs_4_, ...), custom_call_target="tpu_custom_call" | custom-call | flops 5000000000 | tf_op jit(solution)/shard_map/grad/pallas_call | solution.py:50
  398.4 4.9 grad.32.refs_0_
  404.7 4.6 grad.33.refs_0_
  409.9 3.3 grad.34.refs_0_
  413.3 4.0 grad.35.refs_0_
  419.4 20.0 %collective-permute-done.20.refs_1_.refs_6_ = bf16[2,256,1024]{2,1,0:T(8,128)(2,1)S(1)} collective-permute-done((bf16[2,256,1024]{2,1,0:T(8,128)(2,1)S(1)}, bf16[2,256,1024]{2,1,0:T(8,128)(2,1)S(1)}, u32[]{:S(2)}, u32[]{:S(2)}) %collective-permute-start.20) | collective-permute-done | bytes 1048608 | tf_op jit(solution)/shard_map/ppermute | solution.py:811
  450.7 5.9 %collective-permute-done.24.refs_4_ = bf16[4,256,256]{2,1,0:T(8,128)(2,1)} collective-permute-done((bf16[4,256,256]{2,1,0:T(8,128)(2,1)}, bf16[4,256,256]{2,1,0:T(8,128)(2,1)}, u32[]{:S(2)}, u32[]{:S(2)}) %collective-permute-start.24) | collective-permute-done | bytes 524320 | tf_op jit(solution)/shard_map/ppermute | solution.py:811
  459.0 3.6 grad.38.refs_0_
  464.5 3.2 grad.39.refs_0_
  469.5 4.7 grad.40.refs_0_
  474.3 8.2 %collective-permute-done.27.refs_6_ = bf16[2,256,384]{2,1,0:T(8,128)(2,1)S(1)} collective-permute-done((bf16[2,256,384]{2,1,0:T(8,128)(2,1)S(1)}, bf16[2,256,384]{2,1,0:T(8,128)(2,1)S(1)}, u32[]{:S(2)}, u32[]{:S(2)}) %collective-permute-start.27) | collective-permute-done | bytes 393248 | tf_op jit(solution)/shard_map/ppermute | solution.py:811
  485.6 3.1 collective-permute-start.32
  488.7 2.9 collective-permute-done.28.refs_1_
  493.9 4.6 grad.42.refs_0_
  498.5 3.8 collective-permute-done.30.refs_1_.refs_8_
  502.3 3.1 grad.43.refs_0_
  509.8 3.0 grad.45.refs_0_
  518.4 3.8 collective-permute-done.35.refs_6_
  526.0 4.6 grad.47
  (246 shorter events, 107.4 us)
Async XLA Ops:
  4.8 30.2 %all-to-all-start = ((bf16[4,2,64,2048]{3,2,1,0:T(8,128)(2,1)}), bf16[4,2,64,2048]{3,2,1,0:T(8,128)(2,1)S(1)}, u32[]{:S(2)}, u32[]{:S(2)}) async-start(bf16[4,2,64,2048]{3,2,1,0:T(8,128)(2,1)} %broadcast_in_dim.10), calls=%async_computation | async-start | bytes 4194304 | tf_op jit(solution)/shard_map/all_to_all | solution.py:823
  17.2 22.9 %copy-start.67 = (f32[64]{0:T(128)S(1)}, f32[64]{0:T(128)}, u32[]{:S(2)}) copy-start(f32[64]{0:T(128)} %param.20) | copy-start | bytes 772
  17.2 23.0 %copy-start.68 = (f32[64]{0:T(128)S(1)}, f32[64]{0:T(128)}, u32[]{:S(2)}) copy-start(f32[64]{0:T(128)} %param.21) | copy-start | bytes 772
  36.4 42.7 %all-to-all-start.1 = ((bf16[4,2,64,2048]{3,2,1,0:T(8,128)(2,1)}), bf16[4,2,64,2048]{3,2,1,0:T(8,128)(2,1)S(1)}, u32[]{:S(2)}, u32[]{:S(2)}) async-start(bf16[4,2,64,2048]{3,2,1,0:T(8,128)(2,1)} %copy-done.1), calls=%async_computation.1 | async-start | bytes 4194304 | tf_op jit(solution)/shard_map/all_to_all | solution.py:823
  40.0 4.6 collective-permute-start
  51.8 27.3 %copy-start.32 = (bf16[2,512,128]{2,1,0:T(8,128)(2,1)}, bf16[2,512,128]{2,1,0:T(8,128)(2,1)S(1)}, u32[]{:S(2)}) copy-start(bf16[2,512,128]{2,1,0:T(8,128)(2,1)S(1)} %get-tuple-element.59.refs_0_.refs_3_.refs_4_) | copy-start | bytes 786436
  51.8 17.7 %collective-permute-start.3 = (bf16[2,512,128]{2,1,0:T(8,128)(2,1)S(1)}, bf16[2,512,128]{2,1,0:T(8,128)(2,1)S(1)}, u32[]{:S(2)}, u32[]{:S(2)}) collective-permute-start(bf16[2,512,128]{2,1,0:T(8,128)(2,1)S(1)} %get-tuple-element.59.refs_0_.refs_3_.refs_4_), channel_id=1, source_target_pairs={{0,20},{1,21},{2,22},{3,23},{4,16},{5,17},{6,18},{7,19},{8,28},{9,... | collective-permute-start | bytes 786440 | tf_op jit(solution)/shard_map/ppermute | solution.py:811
  55.5 23.6 %collective-permute-start.2 = (bf16[2,512,128]{2,1,0:T(8,128)(2,1)S(1)}, bf16[2,512,128]{2,1,0:T(8,128)(2,1)S(1)}, u32[]{:S(2)}, u32[]{:S(2)}) collective-permute-start(bf16[2,512,128]{2,1,0:T(8,128)(2,1)S(1)} %get-tuple-element.59.refs_0_.refs_3_.refs_4_), channel_id=1, source_target_pairs={{0,16},{1,17},{2,18},{3,19},{4,20},{5,21},{6,22},{7,23},{8,24},{9,... | collective-permute-start | bytes 786440 | tf_op jit(solution)/shard_map/ppermute | solution.py:811
  55.8 23.3 %collective-permute-start.1 = (bf16[2,512,128]{2,1,0:T(8,128)(2,1)S(1)}, bf16[2,512,128]{2,1,0:T(8,128)(2,1)S(1)}, u32[]{:S(2)}, u32[]{:S(2)}) collective-permute-start(bf16[2,512,128]{2,1,0:T(8,128)(2,1)S(1)} %get-tuple-element.59.refs_0_.refs_3_.refs_4_), channel_id=1, source_target_pairs={{0,4},{1,5},{2,6},{3,7},{4,0},{5,1},{6,2},{7,3},{8,12},{9,13},{10,... | collective-permute-start | bytes 786440 | tf_op jit(solution)/shard_map/ppermute | solution.py:811
  69.5 20.3 %copy-start.33 = (bf16[2,512,128]{2,1,0:T(8,128)(2,1)}, bf16[2,512,128]{2,1,0:T(8,128)(2,1)S(1)}, u32[]{:S(2)}) copy-start(bf16[2,512,128]{2,1,0:T(8,128)(2,1)S(1)} %collective-permute-done.3.refs_6_.refs_7_) | copy-start | bytes 786436
  79.1 10.8 %copy-start.34 = (bf16[2,512,128]{2,1,0:T(8,128)(2,1)}, bf16[2,512,128]{2,1,0:T(8,128)(2,1)S(1)}, u32[]{:S(2)}) copy-start(bf16[2,512,128]{2,1,0:T(8,128)(2,1)S(1)} %collective-permute-done.2.refs_5_.refs_6_) | copy-start | bytes 786436
  79.1 10.8 %copy-start.35 = (bf16[2,512,128]{2,1,0:T(8,128)(2,1)}, bf16[2,512,128]{2,1,0:T(8,128)(2,1)S(1)}, u32[]{:S(2)}) copy-start(bf16[2,512,128]{2,1,0:T(8,128)(2,1)S(1)} %collective-permute-done.1.refs_4_.refs_5_) | copy-start | bytes 786436
  89.9 8.7 %copy-start.44 = (bf16[4,2,64,256]{3,2,1,0:T(8,128)(2,1)}, bf16[4,2,64,256]{3,2,1,0:T(8,128)(2,1)S(1)}, u32[]{:S(2)}) copy-start(bf16[4,2,64,256]{3,2,1,0:T(8,128)(2,1)S(1)} %get-tuple-element.75.refs_9_) | copy-start | bytes 786436
  89.9 8.7 %copy-start.48 = (bf16[4,2,64,256]{3,2,1,0:T(8,128)(2,1)}, bf16[4,2,64,256]{3,2,1,0:T(8,128)(2,1)S(1)}, u32[]{:S(2)}) copy-start(bf16[4,2,64,256]{3,2,1,0:T(8,128)(2,1)S(1)} %get-tuple-element.76.refs_10_) | copy-start | bytes 786436
  89.9 4.4 collective-permute-start.4
  99.9 29.3 %all-to-all-start.2 = ((bf16[4,2,64,2048]{3,2,1,0:T(8,128)(2,1)}), bf16[4,2,64,2048]{3,2,1,0:T(8,128)(2,1)S(1)}, u32[]{:S(2)}, u32[]{:S(2)}) async-start(bf16[4,2,64,2048]{3,2,1,0:T(8,128)(2,1)} %bitcast.59), calls=%async_computation.2 | async-start | bytes 4194304 | tf_op jit(solution)/shard_map/all_to_all | solution.py:823
  103.7 4.4 collective-permute-start.5
  109.5 19.8 %copy-start.36 = (f32[2048]{0:T(1024)S(1)}, f32[2048]{0:T(1024)}, u32[]{:S(2)}) copy-start(f32[2048]{0:T(1024)} %param.23) | copy-start | bytes 24580
  132.6 28.0 %copy-start = (bf16[4,2,64,2048]{3,2,1,0:T(8,128)(2,1)}, bf16[4,2,64,2048]{3,2,1,0:T(8,128)(2,1)S(1)}, u32[]{:S(2)}) copy-start(bf16[4,2,64,2048]{3,2,1,0:T(8,128)(2,1)S(1)} %get-tuple-element.64.refs_0_) | copy-start | bytes 6291460
  132.6 28.0 %copy-start.55 = (f32[2,64,2048]{2,1,0:T(8,128)}, f32[2,64,2048]{2,1,0:T(8,128)S(1)}, u32[]{:S(2)}) copy-start(f32[2,64,2048]{2,1,0:T(8,128)S(1)} %get-tuple-element.70.refs_2_) | copy-start | bytes 3145732
  160.6 4.2 collective-permute-start.6
  198.8 6.7 %collective-permute-start.7 = (bf16[512,2048]{1,0:T(8,128)(2,1)}, bf16[512,2048]{1,0:T(8,128)(2,1)S(1)}, u32[]{:S(2)}, u32[]{:S(2)}) collective-permute-start(bf16[512,2048]{1,0:T(8,128)(2,1)} %get-tuple-element.65.refs_0_), channel_id=1, source_target_pairs={{0,1},{1,0},{2,3},{3,2},{4,5},{5,4},{6,7},{7,6},{8,9},{9,8},{10,11... | collective-permute-start | bytes 6291464 | tf_op jit(solution)/shard_map/ppermute | solution.py:811
  209.6 39.3 %all-to-all-start.4 = ((bf16[4,2,64,2048]{3,2,1,0:T(8,128)(2,1)}), bf16[4,2,64,2048]{3,2,1,0:T(8,128)(2,1)S(1)}, u32[]{:S(2)}, u32[]{:S(2)}) async-start(bf16[4,2,64,2048]{3,2,1,0:T(8,128)(2,1)} %bitcast.58), calls=%async_computation.4 | async-start | bytes 4194304 | tf_op jit(solution)/shard_map/all_to_all | solution.py:823
  214.3 48.8 %collective-permute-start.9 = (bf16[4,256,1024]{2,1,0:T(8,128)(2,1)}, bf16[4,256,1024]{2,1,0:T(8,128)(2,1)}, u32[]{:S(2)}, u32[]{:S(2)}) collective-permute-start(bf16[4,256,1024]{2,1,0:T(8,128)(2,1)} %grad.24.refs_0_), channel_id=1, source_target_pairs={{0,4},{1,5},{2,6},{3,7},{4,0},{5,1},{6,2},{7,3},{8,12},{9,13},{10,... | collective-permute-start | bytes 6291464 | tf_op jit(solution)/shard_map/ppermute | solution.py:811
  228.0 41.7 %collective-permute-start.8 = (bf16[4,256,384]{2,1,0:T(8,128)(2,1)}, bf16[4,256,384]{2,1,0:T(8,128)(2,1)}, u32[]{:S(2)}, u32[]{:S(2)}) collective-permute-start(bf16[4,256,384]{2,1,0:T(8,128)(2,1)} %grad.25.refs_0_), channel_id=1, source_target_pairs={{0,16},{1,17},{2,18},{3,19},{4,20},{5,21},{6,22},{7,23},{8,24},{9,... | collective-permute-start | bytes 2359304 | tf_op jit(solution)/shard_map/ppermute | solution.py:811
  255.3 44.1 %all-to-all-start.5 = ((bf16[4,2,64,2048]{3,2,1,0:T(8,128)(2,1)}), bf16[4,2,64,2048]{3,2,1,0:T(8,128)(2,1)}, u32[]{:S(2)}, u32[]{:S(2)}) async-start(bf16[4,2,64,2048]{3,2,1,0:T(8,128)(2,1)} %get-tuple-element.71.refs_0_), calls=%async_computation.5 | async-start | bytes 4194304 | tf_op jit(solution)/shard_map/all_to_all | solution.py:823
  272.8 10.2 %copy-start.25 = (bf16[4,256,256]{2,1,0:T(8,128)(2,1)S(1)}, bf16[4,256,256]{2,1,0:T(8,128)(2,1)}, u32[]{:S(2)}) copy-start(bf16[4,256,256]{2,1,0:T(8,128)(2,1)} %copy-done.24) | copy-start | bytes 1572868
  283.1 16.4 %collective-permute-start.10 = (bf16[512,2048]{1,0:T(8,128)(2,1)}, bf16[512,2048]{1,0:T(8,128)(2,1)S(1)}, u32[]{:S(2)}, u32[]{:S(2)}) collective-permute-start(bf16[512,2048]{1,0:T(8,128)(2,1)} %get-tuple-element.72.refs_0_), channel_id=1, source_target_pairs={{0,1},{1,0},{2,3},{3,2},{4,5},{5,4},{6,7},{7,6},{8,9},{9,8},{10,11... | collective-permute-start | bytes 6291464 | tf_op jit(solution)/shard_map/ppermute | solution.py:811
  283.1 14.3 %collective-permute-start.11 = (bf16[4,256,256]{2,1,0:T(8,128)(2,1)S(1)}, bf16[4,256,256]{2,1,0:T(8,128)(2,1)S(1)}, u32[]{:S(2)}, u32[]{:S(2)}) collective-permute-start(bf16[4,256,256]{2,1,0:T(8,128)(2,1)S(1)} %copy-done.25), channel_id=1, source_target_pairs={{0,4},{1,5},{2,6},{3,7},{4,0},{5,1},{6,2},{7,3},{8,12},{9,13},{10,... | collective-permute-start | bytes 1572872 | tf_op jit(solution)/shard_map/ppermute | solution.py:811
  283.8 14.9 %collective-permute-start.12 = (bf16[2,256,256]{2,1,0:T(8,128)(2,1)S(1)}, bf16[2,256,256]{2,1,0:T(8,128)(2,1)S(1)}, u32[]{:S(2)}, u32[]{:S(2)}) collective-permute-start(bf16[2,256,256]{2,1,0:T(8,128)(2,1)S(1)} %grad.28.refs_0_), channel_id=1, source_target_pairs={{0,16},{1,17},{2,18},{3,19},{4,20},{5,21},{6,22},{7,23},{8,24},{9,... | collective-permute-start | bytes 786440 | tf_op jit(solution)/shard_map/ppermute | solution.py:811
  297.4 7.3 %copy-start.21 = (bf16[4,256,256]{2,1,0:T(8,128)(2,1)}, bf16[4,256,256]{2,1,0:T(8,128)(2,1)S(1)}, u32[]{:S(2)}) copy-start(bf16[4,256,256]{2,1,0:T(8,128)(2,1)S(1)} %collective-permute-done.11.refs_4_) | copy-start | bytes 1572868
  299.4 11.1 %collective-permute-start.13 = (bf16[4,2,64,2048]{3,2,1,0:T(8,128)(2,1)}, bf16[4,2,64,2048]{3,2,1,0:T(8,128)(2,1)}, u32[]{:S(2)}, u32[]{:S(2)}) collective-permute-start(bf16[4,2,64,2048]{3,2,1,0:T(8,128)(2,1)} %all-to-all-done.5.refs_1_), channel_id=1, source_target_pairs={{0,1},{1,0},{2,3},{3,2},{4,5},{5,4},{6,7},{7,6},{8,9},{9,8},{10,11... | collective-permute-start | bytes 6291464 | tf_op jit(solution)/shard_map/ppermute | solution.py:811
  299.4 37.1 %collective-permute-start.14 = (bf16[4,256,768]{2,1,0:T(8,128)(2,1)}, bf16[4,256,768]{2,1,0:T(8,128)(2,1)}, u32[]{:S(2)}, u32[]{:S(2)}) collective-permute-start(bf16[4,256,768]{2,1,0:T(8,128)(2,1)} %grad.27.refs_0_), channel_id=1, source_target_pairs={{0,4},{1,5},{2,6},{3,7},{4,0},{5,1},{6,2},{7,3},{8,12},{9,13},{10,... | collective-permute-start | bytes 4718600 | tf_op jit(solution)/shard_map/ppermute | solution.py:811
  300.9 36.9 %collective-permute-start.15 = (bf16[2,256,768]{2,1,0:T(8,128)(2,1)}, bf16[2,256,768]{2,1,0:T(8,128)(2,1)}, u32[]{:S(2)}, u32[]{:S(2)}) collective-permute-start(bf16[2,256,768]{2,1,0:T(8,128)(2,1)} %copy-done.16), channel_id=1, source_target_pairs={{0,16},{1,17},{2,18},{3,19},{4,20},{5,21},{6,22},{7,23},{8,24},{9,... | collective-permute-start | bytes 2359304 | tf_op jit(solution)/shard_map/ppermute | solution.py:811
  306.0 66.9 %all-to-all-start.6 = ((bf16[4,2,64,2048]{3,2,1,0:T(8,128)(2,1)}), bf16[4,2,64,2048]{3,2,1,0:T(8,128)(2,1)S(1)}, u32[]{:S(2)}, u32[]{:S(2)}) async-start(bf16[4,2,64,2048]{3,2,1,0:T(8,128)(2,1)} %bitcast.56), calls=%async_computation.6 | async-start | bytes 4194304 | tf_op jit(solution)/shard_map/all_to_all | solution.py:823
  337.8 10.3 %collective-permute-start.16 = (bf16[2,512,128]{2,1,0:T(8,128)(2,1)S(1)}, bf16[2,512,128]{2,1,0:T(8,128)(2,1)S(1)}, u32[]{:S(2)}, u32[]{:S(2)}) collective-permute-start(bf16[2,512,128]{2,1,0:T(8,128)(2,1)S(1)} %get-tuple-element.85), channel_id=1, source_target_pairs={{0,4},{1,5},{2,6},{3,7},{4,0},{5,1},{6,2},{7,3},{8,12},{9,13},{10,... | collective-permute-start | bytes 786440 | tf_op jit(solution)/shard_map/ppermute | solution.py:811
  339.2 20.9 %collective-permute-start.17 = (bf16[2,512,128]{2,1,0:T(8,128)(2,1)S(1)}, bf16[2,512,128]{2,1,0:T(8,128)(2,1)S(1)}, u32[]{:S(2)}, u32[]{:S(2)}) collective-permute-start(bf16[2,512,128]{2,1,0:T(8,128)(2,1)S(1)} %get-tuple-element.86), channel_id=1, source_target_pairs={{0,16},{1,17},{2,18},{3,19},{4,20},{5,21},{6,22},{7,23},{8,24},{9,... | collective-permute-start | bytes 786440 | tf_op jit(solution)/shard_map/ppermute | solution.py:811
  339.2 25.8 %collective-permute-start.18 = (bf16[2,512,128]{2,1,0:T(8,128)(2,1)S(1)}, bf16[2,512,128]{2,1,0:T(8,128)(2,1)S(1)}, u32[]{:S(2)}, u32[]{:S(2)}) collective-permute-start(bf16[2,512,128]{2,1,0:T(8,128)(2,1)S(1)} %get-tuple-element.87), channel_id=1, source_target_pairs={{0,20},{1,21},{2,22},{3,23},{4,16},{5,17},{6,18},{7,19},{8,28},{9,... | collective-permute-start | bytes 786440 | tf_op jit(solution)/shard_map/ppermute | solution.py:811
  372.9 4.5 collective-permute-start.19
  381.3 59.1 %all-to-all-start.7 = ((bf16[4,2,64,2048]{3,2,1,0:T(8,128)(2,1)}), bf16[4,2,64,2048]{3,2,1,0:T(8,128)(2,1)S(1)}, u32[]{:S(2)}, u32[]{:S(2)}) async-start(bf16[4,2,64,2048]{3,2,1,0:T(8,128)(2,1)} %bitcast.57), calls=%async_computation.7 | async-start | bytes 4194304 | tf_op jit(solution)/shard_map/all_to_all | solution.py:823
  390.3 8.1 %copy-start.40 = (bf16[4,2,64,384]{3,2,1,0:T(8,128)(2,1)S(1)}, bf16[4,2,64,384]{3,2,1,0:T(8,128)(2,1)}, u32[]{:S(2)}) copy-start(bf16[4,2,64,384]{3,2,1,0:T(8,128)(2,1)} %get-tuple-element.91) | copy-start | bytes 1179652
  390.3 8.1 %copy-start.42 = (bf16[4,2,64,384]{3,2,1,0:T(8,128)(2,1)S(1)}, bf16[4,2,64,384]{3,2,1,0:T(8,128)(2,1)}, u32[]{:S(2)}) copy-start(bf16[4,2,64,384]{3,2,1,0:T(8,128)(2,1)} %get-tuple-element.92) | copy-start | bytes 1179652
  390.3 49.1 %collective-permute-start.20 = (bf16[2,256,1024]{2,1,0:T(8,128)(2,1)S(1)}, bf16[2,256,1024]{2,1,0:T(8,128)(2,1)S(1)}, u32[]{:S(2)}, u32[]{:S(2)}) collective-permute-start(bf16[2,256,1024]{2,1,0:T(8,128)(2,1)S(1)} %grad.30.refs_0_), channel_id=1, source_target_pairs={{0,16},{1,17},{2,18},{3,19},{4,20},{5,21},{6,22},{7,23},{8,24},{9,... | collective-permute-start | bytes 3145736 | tf_op jit(solution)/shard_map/ppermute | solution.py:811
  397.7 61.3 %collective-permute-start.25 = (bf16[4,256,640]{2,1,0:T(8,128)(2,1)}, bf16[4,256,640]{2,1,0:T(8,128)(2,1)}, u32[]{:S(2)}, u32[]{:S(2)}) collective-permute-start(bf16[4,256,640]{2,1,0:T(8,128)(2,1)} %grad.31.refs_0_), channel_id=1, source_target_pairs={{0,4},{1,5},{2,6},{3,7},{4,0},{5,1},{6,2},{7,3},{8,12},{9,13},{10,... | collective-permute-start | bytes 3932168 | tf_op jit(solution)/shard_map/ppermute | solution.py:811
  403.3 43.5 %collective-permute-start.23 = (bf16[4,256,384]{2,1,0:T(8,128)(2,1)}, bf16[4,256,384]{2,1,0:T(8,128)(2,1)}, u32[]{:S(2)}, u32[]{:S(2)}) collective-permute-start(bf16[4,256,384]{2,1,0:T(8,128)(2,1)} %grad.32.refs_0_), channel_id=1, source_target_pairs={{0,4},{1,5},{2,6},{3,7},{4,0},{5,1},{6,2},{7,3},{8,12},{9,13},{10,... | collective-permute-start | bytes 2359304 | tf_op jit(solution)/shard_map/ppermute | solution.py:811
  409.3 47.4 %collective-permute-start.24 = (bf16[4,256,256]{2,1,0:T(8,128)(2,1)}, bf16[4,256,256]{2,1,0:T(8,128)(2,1)}, u32[]{:S(2)}, u32[]{:S(2)}) collective-permute-start(bf16[4,256,256]{2,1,0:T(8,128)(2,1)} %grad.33.refs_0_), channel_id=1, source_target_pairs={{0,4},{1,5},{2,6},{3,7},{4,0},{5,1},{6,2},{7,3},{8,12},{9,13},{10,... | collective-permute-start | bytes 1572872 | tf_op jit(solution)/shard_map/ppermute | solution.py:811
  413.2 4.1 collective-permute-start.21
  417.3 52.2 %collective-permute-start.26 = (bf16[1,256,1024]{2,1,0:T(8,128)(2,1)}, bf16[1,256,1024]{2,1,0:T(8,128)(2,1)}, u32[]{:S(2)}, u32[]{:S(2)}) collective-permute-start(bf16[1,256,1024]{2,1,0:T(8,128)(2,1)} %grad.35.refs_0_), channel_id=1, source_target_pairs={{0,8},{1,9},{2,10},{3,11},{4,12},{5,13},{6,14},{7,15},{8,0},{9,1},... | collective-permute-start | bytes 1572872 | tf_op jit(solution)/shard_map/ppermute | solution.py:811
  445.1 11.5 %copy-start.46 = (bf16[4,2,64,256]{3,2,1,0:T(8,128)(2,1)S(1)}, bf16[4,2,64,256]{3,2,1,0:T(8,128)(2,1)}, u32[]{:S(2)}) copy-start(bf16[4,2,64,256]{3,2,1,0:T(8,128)(2,1)} %copy-done.44) | copy-start | bytes 786436
  445.1 11.5 %copy-start.50 = (bf16[4,2,64,256]{3,2,1,0:T(8,128)(2,1)S(1)}, bf16[4,2,64,256]{3,2,1,0:T(8,128)(2,1)}, u32[]{:S(2)}) copy-start(bf16[4,2,64,256]{3,2,1,0:T(8,128)(2,1)} %copy-done.48) | copy-start | bytes 786436
  445.1 29.1 %collective-permute-start.22 = (f32[33,128]{1,0:T(8,128)S(1)}, f32[33,128]{1,0:T(8,128)S(1)}, u32[]{:S(2)}, u32[]{:S(2)}) collective-permute-start(f32[33,128]{1,0:T(8,128)S(1)} %bitcast_add_fusion), channel_id=1, source_target_pairs={{0,2},{1,3},{2,0},{3,1},{4,6},{5,7},{6,4},{7,5},{8,10},{9,11},{10,... | collective-permute-start | bytes 50696 | tf_op jit(solution)/shard_map/ppermute | solution.py:811
  449.4 33.1 %collective-permute-start.27 = (bf16[2,256,384]{2,1,0:T(8,128)(2,1)S(1)}, bf16[2,256,384]{2,1,0:T(8,128)(2,1)S(1)}, u32[]{:S(2)}, u32[]{:S(2)}) collective-permute-start(bf16[2,256,384]{2,1,0:T(8,128)(2,1)S(1)} %grad.36.refs_0_), channel_id=1, source_target_pairs={{0,16},{1,17},{2,18},{3,19},{4,20},{5,21},{6,22},{7,23},{8,24},{9,... | collective-permute-start | bytes 1179656 | tf_op jit(solution)/shard_map/ppermute | solution.py:811
  462.6 39.6 %collective-permute-start.30 = (bf16[2,256,640]{2,1,0:T(8,128)(2,1)S(1)}, bf16[2,256,640]{2,1,0:T(8,128)(2,1)S(1)}, u32[]{:S(2)}, u32[]{:S(2)}) collective-permute-start(bf16[2,256,640]{2,1,0:T(8,128)(2,1)S(1)} %grad.38.refs_0_), channel_id=1, source_target_pairs={{0,16},{1,17},{2,18},{3,19},{4,20},{5,21},{6,22},{7,23},{8,24},{9,... | collective-permute-start | bytes 1966088 | tf_op jit(solution)/shard_map/ppermute | solution.py:811
  467.8 26.1 %collective-permute-start.29 = (bf16[1,256,1024]{2,1,0:T(8,128)(2,1)S(1)}, bf16[1,256,1024]{2,1,0:T(8,128)(2,1)S(1)}, u32[]{:S(2)}, u32[]{:S(2)}) collective-permute-start(bf16[1,256,1024]{2,1,0:T(8,128)(2,1)S(1)} %grad.39.refs_0_), channel_id=1, source_target_pairs={{0,8},{1,9},{2,10},{3,11},{4,12},{5,13},{6,14},{7,15},{8,0},{9,1},... | collective-permute-start | bytes 1572872 | tf_op jit(solution)/shard_map/ppermute | solution.py:811
  474.3 10.4 %copy-start.27 = (bf16[2,256,384]{2,1,0:T(8,128)(2,1)S(1)}, bf16[2,256,384]{2,1,0:T(8,128)(2,1)}, u32[]{:S(2)}) copy-start(bf16[2,256,384]{2,1,0:T(8,128)(2,1)} %copy-done.26) | copy-start | bytes 1179652
  484.6 7.0 %collective-permute-start.28 = (f32[33,128]{1,0:T(8,128)S(1)}, f32[33,128]{1,0:T(8,128)S(1)}, u32[]{:S(2)}, u32[]{:S(2)}) collective-permute-start(f32[33,128]{1,0:T(8,128)S(1)} %fusion.7), channel_id=1, source_target_pairs={{0,8},{1,9},{2,10},{3,11},{4,12},{5,13},{6,14},{7,15},{8,0},{9,1},... | collective-permute-start | bytes 50696 | tf_op jit(solution)/shard_map/ppermute | solution.py:811
  484.7 13.7 %collective-permute-start.31 = (bf16[2,256,384]{2,1,0:T(8,128)(2,1)S(1)}, bf16[2,256,384]{2,1,0:T(8,128)(2,1)S(1)}, u32[]{:S(2)}, u32[]{:S(2)}) collective-permute-start(bf16[2,256,384]{2,1,0:T(8,128)(2,1)S(1)} %copy-done.27), channel_id=1, source_target_pairs={{0,4},{1,5},{2,6},{3,7},{4,0},{5,1},{6,2},{7,3},{8,12},{9,13},{10,... | collective-permute-start | bytes 1179656 | tf_op jit(solution)/shard_map/ppermute | solution.py:811
  485.6 22.2 %collective-permute-start.32 = (bf16[2,256,256]{2,1,0:T(8,128)(2,1)S(1)}, bf16[2,256,256]{2,1,0:T(8,128)(2,1)S(1)}, u32[]{:S(2)}, u32[]{:S(2)}) collective-permute-start(bf16[2,256,256]{2,1,0:T(8,128)(2,1)S(1)} %grad.37.refs_0_), channel_id=1, source_target_pairs={{0,16},{1,17},{2,18},{3,19},{4,20},{5,21},{6,22},{7,23},{8,24},{9,... | collective-permute-start | bytes 786440 | tf_op jit(solution)/shard_map/ppermute | solution.py:811
  491.6 18.2 %collective-permute-start.33 = (bf16[1,256,384]{2,1,0:T(8,128)(2,1)S(1)}, bf16[1,256,384]{2,1,0:T(8,128)(2,1)S(1)}, u32[]{:S(2)}, u32[]{:S(2)}) collective-permute-start(bf16[1,256,384]{2,1,0:T(8,128)(2,1)S(1)} %grad.41.refs_0_), channel_id=1, source_target_pairs={{0,8},{1,9},{2,10},{3,11},{4,12},{5,13},{6,14},{7,15},{8,0},{9,1},... | collective-permute-start | bytes 589832 | tf_op jit(solution)/shard_map/ppermute | solution.py:811
  505.4 19.6 %collective-permute-start.36 = (bf16[1,256,1024]{2,1,0:T(8,128)(2,1)S(1)}, bf16[1,256,1024]{2,1,0:T(8,128)(2,1)S(1)}, u32[]{:S(2)}, u32[]{:S(2)}) collective-permute-start(bf16[1,256,1024]{2,1,0:T(8,128)(2,1)S(1)} %grad.43.refs_0_), channel_id=1, source_target_pairs={{0,8},{1,9},{2,10},{3,11},{4,12},{5,13},{6,14},{7,15},{8,0},{9,1},... | collective-permute-start | bytes 1572872 | tf_op jit(solution)/shard_map/ppermute | solution.py:811
  509.7 12.5 %collective-permute-start.35 = (bf16[1,256,256]{2,1,0:T(8,128)(2,1)S(1)}, bf16[1,256,256]{2,1,0:T(8,128)(2,1)S(1)}, u32[]{:S(2)}, u32[]{:S(2)}) collective-permute-start(bf16[1,256,256]{2,1,0:T(8,128)(2,1)S(1)} %grad.44.refs_0_), channel_id=1, source_target_pairs={{0,8},{1,9},{2,10},{3,11},{4,12},{5,13},{6,14},{7,15},{8,0},{9,1},... | collective-permute-start | bytes 393224 | tf_op jit(solution)/shard_map/ppermute | solution.py:811
  512.8 5.5 %collective-permute-start.34 = (f32[33,128]{1,0:T(8,128)S(1)}, f32[33,128]{1,0:T(8,128)S(1)}, u32[]{:S(2)}, u32[]{:S(2)}) collective-permute-start(f32[33,128]{1,0:T(8,128)S(1)} %add.127), channel_id=1, source_target_pairs={{0,4},{1,5},{2,6},{3,7},{4,0},{5,1},{6,2},{7,3},{8,12},{9,13},{10,... | collective-permute-start | bytes 50696 | tf_op jit(solution)/shard_map/ppermute | solution.py:811
  515.0 7.2 %copy-start.51 = (bf16[4,2,64,256]{3,2,1,0:T(8,128)(2,1)S(1)}, bf16[4,2,64,256]{3,2,1,0:T(8,128)(2,1)}, u32[]{:S(2)}) copy-start(bf16[4,2,64,256]{3,2,1,0:T(8,128)(2,1)} %copy-done.48) | copy-start | bytes 786436
  530.6 4.7 collective-permute-start.37
  (51 other events, 136.6 us)
where the time goes:
time: 546 us; the launch traced here: 537 us
  Pallas kernels  216 us (40%)
  waiting for transfers between devices  166 us (30%)
  starting transfers between devices  71.5 us (13%)
  local copies, waits for them, and re-layouts  50.2 us (9%)
  blocking collectives  28 us (5%)
    pallas_call x44, Pallas kernels, call(): pl.pallas_call(body, grid_spec=pltpu.PrefetchScalarGridSpec(num_scalar_pr...  216 us
    ppermute x38, waiting for transfers between devices, swap(): return lax.ppermute(x, AXES, [(d, d ^ mask) for d in range(count)])  131 us
    unnamed x149, local copies, waits for them, and re-layouts  44 us
    ppermute x38, starting transfers between devices, swap(): return lax.ppermute(x, AXES, [(d, d ^ mask) for d in range(count)])  42.5 us
    all_to_all x7, waiting for transfers between devices, exchange(): lax.all_to_all(x, AXES, 0, 0, tiled=True, axis_index_groups=chip_groups())  34.8 us
    all_to_all x7, starting transfers between devices, exchange(): lax.all_to_all(x, AXES, 0, 0, tiled=True, axis_index_groups=chip_groups())  29 us
    all_to_all x1, blocking collectives, exchange(): lax.all_to_all(x, AXES, 0, 0, tiled=True, axis_index_groups=chip_groups())  28 us
  transfers between devices with their start and end apart: 45, of which 26 were waited for; matrix products, arithmetic and copies ran while one was open for 2% of the time, Pallas kernels for 31%

commit v1 on v0

--- a/solution.py
+++ b/solution.py
@@ -20,7 +20,7 @@
 BF = jnp.bfloat16
 F32 = jnp.float32
 MIB = 2**20
-KERNEL_FLOPS = 5 * 10**9
+KERNEL_FLOPS = 3 * 10**9
 
 NN = (((1,), (0,)), ((), ()))
 NT = (((1,), (1,)), ((), ()))

time: 546 us -> 568 us (1.040)
  waiting for transfers between devices: 166 us -> 180 us
  Pallas kernels: 216 us -> 224 us
  starting transfers between devices: 71.5 us -> 78.4 us
    ppermute x38, waiting for transfers between devices: 131 us -> 149 us  [swap(): return lax.ppermute(x, AXES, [(d, d ^ mask) for d in range(count)])]
    pallas_call x44, Pallas kernels: 216 us -> 224 us  [call(): pl.pallas_call(body, grid_spec=pltpu.PrefetchScalarGridSpec(num_scalar_pr...]
    unnamed x149 -> x169, local copies, waits for them, and re-layouts: 44 us -> 38.9 us
  transfers between devices with their start and end apart: 45 -> 45, of which waited for: 26 -> 25; matrix products, arithmetic and copies ran while one was open for 2% -> 2% of each run, Pallas kernels for 31% -> 30%
where the time goes in v1:
time: 568 us; the launch traced here: 561 us
  Pallas kernels  224 us (39%)
  waiting for transfers between devices  180 us (32%)
  starting transfers between devices  78.4 us (14%)
  local copies, waits for them, and re-layouts  45.1 us (8%)
  blocking collectives  28 us (5%)
    pallas_call x44, Pallas kernels, call(): pl.pallas_call(body, grid_spec=pltpu.PrefetchScalarGridSpec(num_scalar_pr...  224 us
    ppermute x38, waiting for transfers between devices, swap(): return lax.ppermute(x, AXES, [(d, d ^ mask) for d in range(count)])  149 us
    ppermute x38, starting transfers between devices, swap(): return lax.ppermute(x, AXES, [(d, d ^ mask) for d in range(count)])  46.6 us
    unnamed x169, local copies, waits for them, and re-layouts  38.9 us
    all_to_all x7, waiting for transfers between devices, exchange(): lax.all_to_all(x, AXES, 0, 0, tiled=True, axis_index_groups=chip_groups())  31.8 us
    all_to_all x7, starting transfers between devices, exchange(): lax.all_to_all(x, AXES, 0, 0, tiled=True, axis_index_groups=chip_groups())  31.7 us
    all_to_all x1, blocking collectives, exchange(): lax.all_to_all(x, AXES, 0, 0, tiled=True, axis_index_groups=chip_groups())  28 us
  transfers between devices with their start and end apart: 45, of which 25 were waited for; matrix products, arithmetic and copies ran while one was open for 2% of the time, Pallas kernels for 30%

profile of v1, /device:TPU:0, one launch (start us, length us, event | category | flops | bytes accessed | tf_op | source)
XLA Modules:
  0.0 561.1 jit_solution(17538848657987355764)
XLA Ops:
  4.8 5.4 all-to-all-start
  12.5 4.7 prepare.1.refs_0_.refs_3_.refs_10_
  17.2 17.9 %all-to-all-done.refs_1_.refs_8_ = bf16[4,2,64,2048]{3,2,1,0:T(8,128)(2,1)S(1)} async-done(((bf16[4,2,64,2048]{3,2,1,0:T(8,128)(2,1)}), bf16[4,2,64,2048]{3,2,1,0:T(8,128)(2,1)S(1)}, u32[]{:S(2)}, u32[]{:S(2)}) %all-to-all-start) | async-done | bytes 2097184 | tf_op jit(solution)/shard_map/all_to_all | solution.py:823
  35.1 4.5 all-to-all-start.1
  40.2 3.7 collective-permute-done.refs_2_.refs_9_
  43.9 6.5 %project.1 = (bf16[2,512,128]{2,1,0:T(8,128)(2,1)S(1)}, bf16[2,2,64,1024]{3,2,1,0:T(8,128)(2,1)S(1)}, f32[2,2,320,256]{3,2,1,0:T(8,128)}) custom-call(s32[5]{0:T(128)S(1)} %pad_add_fusion.at_ref, bf16[384,2048]{1,0:T(8,128)(2,1)} %prepare.1.refs_0_.refs_3_.refs_10_, bf16[4,2,64,2048]{3,2,1,0:T(8,128)(2,1)} %copy-done.71, ...), custom_call_target="tpu_custom_call" | custom-call | flops 3000000000 | tf_op jit(solution)/shard_map/project/pallas_call | solution.py:50
  51.2 3.6 collective-permute-start.3
  55.6 5.8 %turn.4.refs_0_.refs_1_.refs_2_ = bf16[2048,1024]{1,0:T(8,128)(2,1)} custom-call(s32[5]{0:T(128)S(1)} %pad_add_fusion.at_ref, bf16[2,512,128]{2,1,0:T(8,128)(2,1)S(1)} %get-tuple-element.59.refs_0_.refs_3_.refs_4_, bf16[512,2048]{1,0:T(8,128)(2,1)} %bitcast.87, bf16[512,2048]{1,0:T(8,128)(2,1)} %bitcast.8.refs_2_), custom_call_target="tpu_custom_call" | custom-call | flops 3000000000 | tf_op jit(solution)/shard_map/turn/pallas_call | solution.py:50
  61.4 7.6 %collective-permute-done.3.refs_6_.refs_7_ = bf16[2,512,128]{2,1,0:T(8,128)(2,1)S(1)} collective-permute-done((bf16[2,512,128]{2,1,0:T(8,128)(2,1)S(1)}, bf16[2,512,128]{2,1,0:T(8,128)(2,1)S(1)}, u32[]{:S(2)}, u32[]{:S(2)}) %collective-permute-start.3) | collective-permute-done | bytes 262176 | tf_op jit(solution)/shard_map/ppermute | solution.py:811
  69.0 9.4 %collective-permute-done.2.refs_5_.refs_6_ = bf16[2,512,128]{2,1,0:T(8,128)(2,1)S(1)} collective-permute-done((bf16[2,512,128]{2,1,0:T(8,128)(2,1)S(1)}, bf16[2,512,128]{2,1,0:T(8,128)(2,1)S(1)}, u32[]{:S(2)}, u32[]{:S(2)}) %collective-permute-start.2) | collective-permute-done | bytes 262176 | tf_op jit(solution)/shard_map/ppermute | solution.py:811
  78.4 9.3 %attend.1 = (bf16[4,2,64,2048]{3,2,1,0:T(8,128)(2,1)}, bf16[4,2,64,2048]{3,2,1,0:T(8,128)(2,1)}, bf16[4,2,64,256]{3,2,1,0:T(8,128)(2,1)S(1)}, bf16[4,2,64,256]{3,2,1,0:T(8,128)(2,1)S(1)}, f32[2,2,1,1024]{3,2,1,0:T(1,128)S(1)}) custom-call(s32[5]{0:T(128)S(1)} %pad_add_fusion.at_ref, bf16[2048,1024]{1,0:T(8,128)(2,1)} %turn.4.refs_0_.refs_1_.refs_2_, ...), custom_call_target="tpu_custom_call" | custom-call | flops 3000000000 | tf_op jit(solution)/shard_map/attend/pallas_call | solution.py:50
  87.9 4.4 collective-permute-done.4
  97.8 3.7 all-to-all-start.2
  102.0 4.1 collective-permute-done.5
  107.4 5.8 %turn.5.refs_0_.refs_1_.refs_2_ = bf16[2048,1024]{1,0:T(8,128)(2,1)} custom-call(s32[5]{0:T(128)S(1)} %pad_add_fusion.at_ref, bf16[512,2048]{1,0:T(8,128)(2,1)} %copy-done.10, bf16[512,2048]{1,0:T(8,128)(2,1)} %bitcast.11.refs_1_.refs_3_, bf16[512,2048]{1,0:T(8,128)(2,1)} %bitcast.93), custom_call_target="tpu_custom_call" | custom-call | flops 3000000000 | tf_op jit(solution)/shard_map/turn/pallas_call | solution.py:50
  113.2 13.9 %all-to-all-done.2.refs_1_ = bf16[4,2,64,2048]{3,2,1,0:T(8,128)(2,1)S(1)} async-done(((bf16[4,2,64,2048]{3,2,1,0:T(8,128)(2,1)}), bf16[4,2,64,2048]{3,2,1,0:T(8,128)(2,1)S(1)}, u32[]{:S(2)}, u32[]{:S(2)}) %all-to-all-start.2) | async-done | bytes 2097184 | tf_op jit(solution)/shard_map/all_to_all | solution.py:823
  130.5 28.0 %all_to_all.40 = bf16[4,2,64,2048]{3,2,1,0:T(8,128)(2,1)S(1)} all-to-all(bf16[4,2,64,2048]{3,2,1,0:T(8,128)(2,1)S(1)} %get-tuple-element.64.refs_0_), channel_id=1, replica_groups={{0,2,8,10},{1,3,9,11},{4,6,12,14},{5,7,13,15},{16,18,24,26},{17,19,25,2..., dimensions={0} | all-to-all | bytes 4194304 | tf_op jit(solution)/shard_map/all_to_all | solution.py:823
  158.5 4.1 collective-permute-done.6
  164.0 32.7 %ffn.1 = (bf16[512,2048]{1,0:T(8,128)(2,1)}, bf16[512,2048]{1,0:T(8,128)(2,1)}, bf16[1024,1024]{1,0:T(8,128)(2,1)}, bf16[1024,1024]{1,0:T(8,128)(2,1)}, bf16[1024,1024]{1,0:T(8,128)(2,1)}) custom-call(s32[5]{0:T(128)S(1)} %pad_add_fusion.at_ref, bf16[4,2,64,2048]{3,2,1,0:T(8,128)(2,1)} %copy-done.1, bf16[512,2048]{1,0:T(8,128)(2,1)} %bitcast.88, ...), custom_call_target="tpu_custom_call" | custom-call | flops 3000000000 | tf_op jit(solution)/shard_map/ffn/pallas_call | solution.py:50
  196.9 6.6 %grad.24.refs_0_ = bf16[4,256,1024]{2,1,0:T(8,128)(2,1)} custom-call(s32[5]{0:T(128)S(1)} %pad_add_fusion.at_ref, bf16[512,2048]{1,0:T(8,128)(2,1)} %get-tuple-element.65.refs_0_, bf16[2048,1024]{1,0:T(8,128)(2,1)} %turn.5.refs_0_.refs_1_.refs_2_, bf16[1024,1024]{1,0:T(8,128)(2,1)} %get-tuple-element.66.refs_2_.refs_3_.refs_4_.refs_1_, ...), custom_call_target="tpu_custom_call" | custom-call | flops 3000000000 | tf_op jit(solution)/shard_map/grad/pallas_call | solution.py:50
  207.4 4.6 all-to-all-start.4
  212.0 2.9 collective-permute-start.9
  216.0 5.8 %turn.6.refs_0_.refs_1_.refs_2_ = bf16[2048,1024]{1,0:T(8,128)(2,1)} custom-call(s32[5]{0:T(128)S(1)} %pad_add_fusion.at_ref, bf16[512,2048]{1,0:T(8,128)(2,1)} %copy-done.9, bf16[512,2048]{1,0:T(8,128)(2,1)} %bitcast.89, bf16[512,2048]{1,0:T(8,128)(2,1)} %bitcast.92), custom_call_target="tpu_custom_call" | custom-call | flops 3000000000 | tf_op jit(solution)/shard_map/turn/pallas_call | solution.py:50
  221.8 5.6 grad.25.refs_0_
  227.4 9.4 %collective-permute-start.8 = (bf16[4,256,384]{2,1,0:T(8,128)(2,1)}, bf16[4,256,384]{2,1,0:T(8,128)(2,1)S(1)}, u32[]{:S(2)}, u32[]{:S(2)}) collective-permute-start(bf16[4,256,384]{2,1,0:T(8,128)(2,1)} %grad.25.refs_0_), channel_id=1, source_target_pairs={{0,16},{1,17},{2,18},{3,19},{4,20},{5,21},{6,22},{7,23},{8,24},{9,... | collective-permute-start | bytes 2359304 | tf_op jit(solution)/shard_map/ppermute | solution.py:811
  236.7 4.3 grad.26.refs_0_
  241.0 6.0 %grad.27.refs_0_ = bf16[4,256,768]{2,1,0:T(8,128)(2,1)} custom-call(s32[5]{0:T(128)S(1)} %pad_add_fusion.at_ref, bf16[4,256,256]{2,1,0:T(8,128)(2,1)S(1)} %grad.26.refs_0_, bf16[2048,1024]{1,0:T(8,128)(2,1)} %turn.6.refs_0_.refs_1_.refs_2_, bf16[1024,1024]{1,0:T(8,128)(2,1)} %get-tuple-element.69.refs_2_.refs_3_, ...), custom_call_target="tpu_custom_call" | custom-call | flops 3000000000 | tf_op jit(solution)/shard_map/grad/pallas_call | solution.py:50
  250.5 4.5 middle_back.1
  256.6 4.5 all-to-all-start.5
  261.1 10.6 %collective-permute-done.8.refs_1_.refs_4_.refs_5_ = bf16[4,256,384]{2,1,0:T(8,128)(2,1)S(1)} collective-permute-done((bf16[4,256,384]{2,1,0:T(8,128)(2,1)}, bf16[4,256,384]{2,1,0:T(8,128)(2,1)S(1)}, u32[]{:S(2)}, u32[]{:S(2)}) %collective-permute-start.8) | collective-permute-done | bytes 786464 | tf_op jit(solution)/shard_map/ppermute | solution.py:811
  271.7 3.1 grad.28.refs_0_
  274.8 10.2 %down.1 = (bf16[512,2048]{1,0:T(8,128)(2,1)}, bf16[512,2048]{1,0:T(8,128)(2,1)}) custom-call(s32[5]{0:T(128)S(1)} %pad_add_fusion.at_ref, bf16[2,256,256]{2,1,0:T(8,128)(2,1)S(1)} %grad.28.refs_0_, bf16[1024,1024]{1,0:T(8,128)(2,1)} %get-tuple-element.66.refs_2_.refs_3_.refs_4_.refs_1_, bf16[2048,2048]{1,0:T(8,128)(2,1)} %refs_2_.3), custom_call_target="tpu_custom_call" | custom-call | flops 3000000000 | tf_op jit(solution)/shard_map/down/pallas_call | solution.py:50
  285.7 3.6 grad.29.refs_0_
  289.3 10.0 %collective-permute-done.11.refs_4_ = bf16[4,256,256]{2,1,0:T(8,128)(2,1)S(1)} collective-permute-done((bf16[4,256,256]{2,1,0:T(8,128)(2,1)S(1)}, bf16[4,256,256]{2,1,0:T(8,128)(2,1)S(1)}, u32[]{:S(2)}, u32[]{:S(2)}) %collective-permute-start.11) | collective-permute-done | bytes 524320 | tf_op jit(solution)/shard_map/ppermute | solution.py:811
  309.5 4.5 all-to-all-start.6
  315.5 14.7 %attend_back.1 = (bf16[4,2,64,256]{3,2,1,0:T(8,128)(2,1)S(1)}, bf16[4,2,64,256]{3,2,1,0:T(8,128)(2,1)S(1)}, bf16[2,512,128]{2,1,0:T(8,128)(2,1)S(1)}, bf16[2,512...) custom-call(s32[5]{0:T(128)S(1)} %pad_add_fusion.at_ref, ...), custom_call_target="tpu_custom_call" | custom-call | flops 3000000000 | tf_op jit(solution)/shard_map/attend_back/pallas_call | solution.py:50
  330.3 9.2 %collective-permute-done.14.refs_5_ = bf16[4,256,768]{2,1,0:T(8,128)(2,1)} collective-permute-done((bf16[4,256,768]{2,1,0:T(8,128)(2,1)}, bf16[4,256,768]{2,1,0:T(8,128)(2,1)}, u32[]{:S(2)}, u32[]{:S(2)}) %collective-permute-start.14) | collective-permute-done | bytes 1572896 | tf_op jit(solution)/shard_map/ppermute | solution.py:811
  341.8 5.9 %collective-permute-start.17 = (bf16[2,512,128]{2,1,0:T(8,128)(2,1)S(1)}, bf16[2,512,128]{2,1,0:T(8,128)(2,1)S(1)}, u32[]{:S(2)}, u32[]{:S(2)}) collective-permute-start(bf16[2,512,128]{2,1,0:T(8,128)(2,1)S(1)} %get-tuple-element.86), channel_id=1, source_target_pairs={{0,16},{1,17},{2,18},{3,19},{4,20},{5,21},{6,22},{7,23},{8,24},{9,... | collective-permute-start | bytes 786440 | tf_op jit(solution)/shard_map/ppermute | solution.py:811
  349.1 5.9 %turn.7.refs_0_.refs_1_ = bf16[2048,1024]{1,0:T(8,128)(2,1)} custom-call(s32[5]{0:T(128)S(1)} %pad_add_fusion.at_ref, bf16[4,2,64,256]{3,2,1,0:T(8,128)(2,1)S(1)} %get-tuple-element.79.refs_0_.refs_5_, bf16[512,2048]{1,0:T(8,128)(2,1)} %bitcast.19.refs_1_, bf16[512,2048]{1,0:T(8,128)(2,1)} %bitcast.20.refs_2_), custom_call_target="tpu_custom_call" | custom-call | flops 3000000000 | tf_op jit(solution)/shard_map/turn/pallas_call | solution.py:50
  355.0 11.2 %collective-permute-done.17.refs_3_ = bf16[2,512,128]{2,1,0:T(8,128)(2,1)S(1)} collective-permute-done((bf16[2,512,128]{2,1,0:T(8,128)(2,1)S(1)}, bf16[2,512,128]{2,1,0:T(8,128)(2,1)S(1)}, u32[]{:S(2)}, u32[]{:S(2)}) %collective-permute-start.17) | collective-permute-done | bytes 262176 | tf_op jit(solution)/shard_map/ppermute | solution.py:811
  366.1 6.0 %collective-permute-done.18.refs_4_ = bf16[2,512,128]{2,1,0:T(8,128)(2,1)S(1)} collective-permute-done((bf16[2,512,128]{2,1,0:T(8,128)(2,1)S(1)}, bf16[2,512,128]{2,1,0:T(8,128)(2,1)S(1)}, u32[]{:S(2)}, u32[]{:S(2)}) %collective-permute-start.18) | collective-permute-done | bytes 262176 | tf_op jit(solution)/shard_map/ppermute | solution.py:811
  372.2 7.9 %project_back.1 = (bf16[4,2,64,2048]{3,2,1,0:T(8,128)(2,1)}, bf16[4,2,64,2048]{3,2,1,0:T(8,128)(2,1)}, bf16[4,2,64,384]{3,2,1,0:T(8,128)(2,1)}, bf16[4,2,64,384]...) custom-call(s32[5]{0:T(128)S(1)} %pad_add_fusion.at_ref, bf16[2048,1024]{1,0:T(8,128)(2,1)} %turn.7.refs_0_.refs_1_, ...), custom_call_target="tpu_custom_call" | custom-call | flops 3000000000 | tf_op jit(solution)/shard_map/project_back/pallas_call | solution.py:50
  384.6 4.1 chip_sum.7.refs_0_
  388.7 4.6 all-to-all-start.7
  393.7 3.9 grad.30.refs_0_
  399.6 6.0 %grad.31.refs_0_ = bf16[4,256,640]{2,1,0:T(8,128)(2,1)} custom-call(s32[5]{0:T(128)S(1)} %pad_add_fusion.at_ref, bf16[2,256,1024]{2,1,0:T(8,128)(2,1)S(1)} %grad.30.refs_0_, bf16[2048,1024]{1,0:T(8,128)(2,1)} %turn.6.refs_0_.refs_1_.refs_2_, bf16[1024,1024]{1,0:T(8,128)(2,1)} %get-tuple-element.68.refs_2_.refs_3_.refs_4_, ...), custom_call_target="tpu_custom_call" | custom-call | flops 3000000000 | tf_op jit(solution)/shard_map/grad/pallas_call | solution.py:50
  406.0 4.9 grad.32.refs_0_
  412.6 4.6 grad.33.refs_0_
  417.2 3.8 grad.34.refs_0_
  421.4 3.9 grad.35.refs_0_
  426.9 19.4 %collective-permute-done.20.refs_1_.refs_6_ = bf16[2,256,1024]{2,1,0:T(8,128)(2,1)S(1)} collective-permute-done((bf16[2,256,1024]{2,1,0:T(8,128)(2,1)S(1)}, bf16[2,256,1024]{2,1,0:T(8,128)(2,1)S(1)}, u32[]{:S(2)}, u32[]{:S(2)}) %collective-permute-start.20) | collective-permute-done | bytes 1048608 | tf_op jit(solution)/shard_map/ppermute | solution.py:811
  450.0 2.9 finish_tokens.1.refs_0_
  459.1 13.7 %collective-permute-done.24.refs_4_ = bf16[4,256,256]{2,1,0:T(8,128)(2,1)} collective-permute-done((bf16[4,256,256]{2,1,0:T(8,128)(2,1)}, bf16[4,256,256]{2,1,0:T(8,128)(2,1)}, u32[]{:S(2)}, u32[]{:S(2)}) %collective-permute-start.24) | collective-permute-done | bytes 524320 | tf_op jit(solution)/shard_map/ppermute | solution.py:811
  476.4 3.6 grad.38.refs_0_
  481.7 3.2 grad.39.refs_0_
  487.4 4.7 grad.40.refs_0_
  492.1 16.1 %collective-permute-done.27.refs_6_ = bf16[2,256,384]{2,1,0:T(8,128)(2,1)S(1)} collective-permute-done((bf16[2,256,384]{2,1,0:T(8,128)(2,1)S(1)}, bf16[2,256,384]{2,1,0:T(8,128)(2,1)S(1)}, u32[]{:S(2)}, u32[]{:S(2)}) %collective-permute-start.27) | collective-permute-done | bytes 393248 | tf_op jit(solution)/shard_map/ppermute | solution.py:811
  511.2 2.9 collective-permute-done.28.refs_1_
  514.3 4.6 grad.42.refs_0_
  518.9 9.2 %collective-permute-done.30.refs_1_.refs_8_ = bf16[2,256,640]{2,1,0:T(8,128)(2,1)S(1)} collective-permute-done((bf16[2,256,640]{2,1,0:T(8,128)(2,1)S(1)}, bf16[2,256,640]{2,1,0:T(8,128)(2,1)S(1)}, u32[]{:S(2)}, u32[]{:S(2)}) %collective-permute-start.30) | collective-permute-done | bytes 655392 | tf_op jit(solution)/shard_map/ppermute | solution.py:811
  528.1 3.1 grad.43.refs_0_
  535.3 3.0 grad.45.refs_0_
  543.3 3.3 collective-permute-done.35.refs_6_
  550.4 4.6 grad.47
  (266 shorter events, 97.2 us)
Async XLA Ops:
  4.8 30.2 %all-to-all-start = ((bf16[4,2,64,2048]{3,2,1,0:T(8,128)(2,1)}), bf16[4,2,64,2048]{3,2,1,0:T(8,128)(2,1)S(1)}, u32[]{:S(2)}, u32[]{:S(2)}) async-start(bf16[4,2,64,2048]{3,2,1,0:T(8,128)(2,1)} %broadcast_in_dim.10), calls=%async_computation | async-start | bytes 4194304 | tf_op jit(solution)/shard_map/all_to_all | solution.py:823
  17.2 22.4 %copy-start.77 = (f32[64]{0:T(128)S(1)}, f32[64]{0:T(128)}, u32[]{:S(2)}) copy-start(f32[64]{0:T(128)} %param.20) | copy-start | bytes 772
  17.2 22.5 %copy-start.78 = (f32[64]{0:T(128)S(1)}, f32[64]{0:T(128)}, u32[]{:S(2)}) copy-start(f32[64]{0:T(128)} %param.21) | copy-start | bytes 772
  35.1 43.4 %all-to-all-start.1 = ((bf16[4,2,64,2048]{3,2,1,0:T(8,128)(2,1)}), bf16[4,2,64,2048]{3,2,1,0:T(8,128)(2,1)}, u32[]{:S(2)}, u32[]{:S(2)}) async-start(bf16[4,2,64,2048]{3,2,1,0:T(8,128)(2,1)} %copy-done.5), calls=%async_computation.1 | async-start | bytes 4194304 | tf_op jit(solution)/shard_map/all_to_all | solution.py:823
  39.5 4.4 collective-permute-start
  39.7 10.6 %copy-start.36 = (f32[64,1]{1,0:T(8,128)}, f32[64,1]{1,0:T(8,128)S(1)}, u32[]{:S(2)}) copy-start(f32[64,1]{1,0:T(8,128)S(1)} %copy.37.refs_6_.refs_15_) | copy-start | bytes 772
  39.8 10.5 %copy-start.34 = (f32[64,1]{1,0:T(8,128)}, f32[64,1]{1,0:T(8,128)S(1)}, u32[]{:S(2)}) copy-start(f32[64,1]{1,0:T(8,128)S(1)} %copy.38.refs_7_.refs_13_) | copy-start | bytes 772
  51.2 27.2 %copy-start.30 = (bf16[2,512,128]{2,1,0:T(8,128)(2,1)}, bf16[2,512,128]{2,1,0:T(8,128)(2,1)S(1)}, u32[]{:S(2)}) copy-start(bf16[2,512,128]{2,1,0:T(8,128)(2,1)S(1)} %get-tuple-element.59.refs_0_.refs_3_.refs_4_) | copy-start | bytes 786436
  51.2 17.9 %collective-permute-start.3 = (bf16[2,512,128]{2,1,0:T(8,128)(2,1)S(1)}, bf16[2,512,128]{2,1,0:T(8,128)(2,1)S(1)}, u32[]{:S(2)}, u32[]{:S(2)}) collective-permute-start(bf16[2,512,128]{2,1,0:T(8,128)(2,1)S(1)} %get-tuple-element.59.refs_0_.refs_3_.refs_4_), channel_id=1, source_target_pairs={{0,20},{1,21},{2,22},{3,23},{4,16},{5,17},{6,18},{7,19},{8,28},{9,... | collective-permute-start | bytes 786440 | tf_op jit(solution)/shard_map/ppermute | solution.py:811
  54.8 23.6 %collective-permute-start.2 = (bf16[2,512,128]{2,1,0:T(8,128)(2,1)S(1)}, bf16[2,512,128]{2,1,0:T(8,128)(2,1)S(1)}, u32[]{:S(2)}, u32[]{:S(2)}) collective-permute-start(bf16[2,512,128]{2,1,0:T(8,128)(2,1)S(1)} %get-tuple-element.59.refs_0_.refs_3_.refs_4_), channel_id=1, source_target_pairs={{0,16},{1,17},{2,18},{3,19},{4,20},{5,21},{6,22},{7,23},{8,24},{9,... | collective-permute-start | bytes 786440 | tf_op jit(solution)/shard_map/ppermute | solution.py:811
  55.1 23.3 %collective-permute-start.1 = (bf16[2,512,128]{2,1,0:T(8,128)(2,1)S(1)}, bf16[2,512,128]{2,1,0:T(8,128)(2,1)S(1)}, u32[]{:S(2)}, u32[]{:S(2)}) collective-permute-start(bf16[2,512,128]{2,1,0:T(8,128)(2,1)S(1)} %get-tuple-element.59.refs_0_.refs_3_.refs_4_), channel_id=1, source_target_pairs={{0,4},{1,5},{2,6},{3,7},{4,0},{5,1},{6,2},{7,3},{8,12},{9,13},{10,... | collective-permute-start | bytes 786440 | tf_op jit(solution)/shard_map/ppermute | solution.py:811
  69.0 18.7 %copy-start.31 = (bf16[2,512,128]{2,1,0:T(8,128)(2,1)}, bf16[2,512,128]{2,1,0:T(8,128)(2,1)S(1)}, u32[]{:S(2)}) copy-start(bf16[2,512,128]{2,1,0:T(8,128)(2,1)S(1)} %collective-permute-done.3.refs_6_.refs_7_) | copy-start | bytes 786436
  78.4 9.4 %copy-start.32 = (bf16[2,512,128]{2,1,0:T(8,128)(2,1)}, bf16[2,512,128]{2,1,0:T(8,128)(2,1)S(1)}, u32[]{:S(2)}) copy-start(bf16[2,512,128]{2,1,0:T(8,128)(2,1)S(1)} %collective-permute-done.2.refs_5_.refs_6_) | copy-start | bytes 786436
  87.8 4.4 collective-permute-start.4
  97.8 29.3 %all-to-all-start.2 = ((bf16[4,2,64,2048]{3,2,1,0:T(8,128)(2,1)}), bf16[4,2,64,2048]{3,2,1,0:T(8,128)(2,1)S(1)}, u32[]{:S(2)}, u32[]{:S(2)}) async-start(bf16[4,2,64,2048]{3,2,1,0:T(8,128)(2,1)} %bitcast.57), calls=%async_computation.2 | async-start | bytes 4194304 | tf_op jit(solution)/shard_map/all_to_all | solution.py:823
  101.6 4.4 collective-permute-start.5
  101.9 25.2 %copy-start.18 = (bf16[64,2,2048]{2,0,1:T(8,128)(2,1)}, bf16[64,2,2048]{2,0,1:T(8,128)(2,1)S(1)}, u32[]{:S(2)}) copy-start(bf16[64,2,2048]{2,0,1:T(8,128)(2,1)S(1)} %copy.56) | copy-start | bytes 1572868
  107.4 19.7 %copy-start.63 = (f32[2048]{0:T(1024)S(1)}, f32[2048]{0:T(1024)}, u32[]{:S(2)}) copy-start(f32[2048]{0:T(1024)} %param.23) | copy-start | bytes 24580
  130.5 28.0 %copy-start.1 = (bf16[4,2,64,2048]{3,2,1,0:T(8,128)(2,1)}, bf16[4,2,64,2048]{3,2,1,0:T(8,128)(2,1)S(1)}, u32[]{:S(2)}) copy-start(bf16[4,2,64,2048]{3,2,1,0:T(8,128)(2,1)S(1)} %get-tuple-element.64.refs_0_) | copy-start | bytes 6291460
  130.5 28.0 %copy-start.66 = (f32[2,64,2048]{2,1,0:T(8,128)}, f32[2,64,2048]{2,1,0:T(8,128)S(1)}, u32[]{:S(2)}) copy-start(f32[2,64,2048]{2,1,0:T(8,128)S(1)} %get-tuple-element.70.refs_2_) | copy-start | bytes 3145732
  158.5 4.2 collective-permute-start.6
  196.7 6.7 %collective-permute-start.7 = (bf16[512,2048]{1,0:T(8,128)(2,1)}, bf16[512,2048]{1,0:T(8,128)(2,1)S(1)}, u32[]{:S(2)}, u32[]{:S(2)}) collective-permute-start(bf16[512,2048]{1,0:T(8,128)(2,1)} %get-tuple-element.65.refs_0_), channel_id=1, source_target_pairs={{0,1},{1,0},{2,3},{3,2},{4,5},{5,4},{6,7},{7,6},{8,9},{9,8},{10,11... | collective-permute-start | bytes 6291464 | tf_op jit(solution)/shard_map/ppermute | solution.py:811
  207.4 40.5 %all-to-all-start.4 = ((bf16[4,2,64,2048]{3,2,1,0:T(8,128)(2,1)}), bf16[4,2,64,2048]{3,2,1,0:T(8,128)(2,1)}, u32[]{:S(2)}, u32[]{:S(2)}) async-start(bf16[4,2,64,2048]{3,2,1,0:T(8,128)(2,1)} %bitcast.56), calls=%async_computation.4 | async-start | bytes 4194304 | tf_op jit(solution)/shard_map/all_to_all | solution.py:823
  212.0 49.0 %collective-permute-start.9 = (bf16[4,256,1024]{2,1,0:T(8,128)(2,1)S(1)}, bf16[4,256,1024]{2,1,0:T(8,128)(2,1)}, u32[]{:S(2)}, u32[]{:S(2)}) collective-permute-start(bf16[4,256,1024]{2,1,0:T(8,128)(2,1)S(1)} %copy-done.8), channel_id=1, source_target_pairs={{0,4},{1,5},{2,6},{3,7},{4,0},{5,1},{6,2},{7,3},{8,12},{9,13},{10,... | collective-permute-start | bytes 6291464 | tf_op jit(solution)/shard_map/ppermute | solution.py:811
  227.4 44.3 %collective-permute-start.8 = (bf16[4,256,384]{2,1,0:T(8,128)(2,1)}, bf16[4,256,384]{2,1,0:T(8,128)(2,1)S(1)}, u32[]{:S(2)}, u32[]{:S(2)}) collective-permute-start(bf16[4,256,384]{2,1,0:T(8,128)(2,1)} %grad.25.refs_0_), channel_id=1, source_target_pairs={{0,16},{1,17},{2,18},{3,19},{4,20},{5,21},{6,22},{7,23},{8,24},{9,... | collective-permute-start | bytes 2359304 | tf_op jit(solution)/shard_map/ppermute | solution.py:811
  256.6 45.8 %all-to-all-start.5 = ((bf16[4,2,64,2048]{3,2,1,0:T(8,128)(2,1)}), bf16[4,2,64,2048]{3,2,1,0:T(8,128)(2,1)}, u32[]{:S(2)}, u32[]{:S(2)}) async-start(bf16[4,2,64,2048]{3,2,1,0:T(8,128)(2,1)} %get-tuple-element.71.refs_0_), calls=%async_computation.5 | async-start | bytes 4194304 | tf_op jit(solution)/shard_map/all_to_all | solution.py:823
  271.7 145.5 %copy-start.2 = (bf16[4,256,384]{2,1,0:T(8,128)(2,1)}, bf16[4,256,384]{2,1,0:T(8,128)(2,1)S(1)}, u32[]{:S(2)}) copy-start(bf16[4,256,384]{2,1,0:T(8,128)(2,1)S(1)} %collective-permute-done.8.refs_1_.refs_4_.refs_5_) | copy-start | bytes 2359300
  274.8 10.2 %copy-start.58 = (bf16[4,256,256]{2,1,0:T(8,128)(2,1)S(1)}, bf16[4,256,256]{2,1,0:T(8,128)(2,1)}, u32[]{:S(2)}) copy-start(bf16[4,256,256]{2,1,0:T(8,128)(2,1)} %copy-done.57) | copy-start | bytes 1572868
  285.0 16.1 %collective-permute-start.10 = (bf16[512,2048]{1,0:T(8,128)(2,1)}, bf16[512,2048]{1,0:T(8,128)(2,1)S(1)}, u32[]{:S(2)}, u32[]{:S(2)}) collective-permute-start(bf16[512,2048]{1,0:T(8,128)(2,1)} %get-tuple-element.72.refs_0_), channel_id=1, source_target_pairs={{0,1},{1,0},{2,3},{3,2},{4,5},{5,4},{6,7},{7,6},{8,9},{9,8},{10,11... | collective-permute-start | bytes 6291464 | tf_op jit(solution)/shard_map/ppermute | solution.py:811
  285.0 14.3 %collective-permute-start.11 = (bf16[4,256,256]{2,1,0:T(8,128)(2,1)S(1)}, bf16[4,256,256]{2,1,0:T(8,128)(2,1)S(1)}, u32[]{:S(2)}, u32[]{:S(2)}) collective-permute-start(bf16[4,256,256]{2,1,0:T(8,128)(2,1)S(1)} %copy-done.58), channel_id=1, source_target_pairs={{0,4},{1,5},{2,6},{3,7},{4,0},{5,1},{6,2},{7,3},{8,12},{9,13},{10,... | collective-permute-start | bytes 1572872 | tf_op jit(solution)/shard_map/ppermute | solution.py:811
  285.4 14.9 %collective-permute-start.12 = (bf16[2,256,256]{2,1,0:T(8,128)(2,1)S(1)}, bf16[2,256,256]{2,1,0:T(8,128)(2,1)S(1)}, u32[]{:S(2)}, u32[]{:S(2)}) collective-permute-start(bf16[2,256,256]{2,1,0:T(8,128)(2,1)S(1)} %grad.28.refs_0_), channel_id=1, source_target_pairs={{0,16},{1,17},{2,18},{3,19},{4,20},{5,21},{6,22},{7,23},{8,24},{9,... | collective-permute-start | bytes 786440 | tf_op jit(solution)/shard_map/ppermute | solution.py:811
  302.4 11.7 %collective-permute-start.13 = (bf16[4,2,64,2048]{3,2,1,0:T(8,128)(2,1)}, bf16[4,2,64,2048]{3,2,1,0:T(8,128)(2,1)}, u32[]{:S(2)}, u32[]{:S(2)}) collective-permute-start(bf16[4,2,64,2048]{3,2,1,0:T(8,128)(2,1)} %all-to-all-done.5.refs_1_), channel_id=1, source_target_pairs={{0,1},{1,0},{2,3},{3,2},{4,5},{5,4},{6,7},{7,6},{8,9},{9,8},{10,11... | collective-permute-start | bytes 6291464 | tf_op jit(solution)/shard_map/ppermute | solution.py:811
  302.4 37.1 %collective-permute-start.14 = (bf16[4,256,768]{2,1,0:T(8,128)(2,1)}, bf16[4,256,768]{2,1,0:T(8,128)(2,1)}, u32[]{:S(2)}, u32[]{:S(2)}) collective-permute-start(bf16[4,256,768]{2,1,0:T(8,128)(2,1)} %grad.27.refs_0_), channel_id=1, source_target_pairs={{0,4},{1,5},{2,6},{3,7},{4,0},{5,1},{6,2},{7,3},{8,12},{9,13},{10,... | collective-permute-start | bytes 4718600 | tf_op jit(solution)/shard_map/ppermute | solution.py:811
  304.0 36.2 %collective-permute-start.15 = (bf16[2,256,768]{2,1,0:T(8,128)(2,1)S(1)}, bf16[2,256,768]{2,1,0:T(8,128)(2,1)S(1)}, u32[]{:S(2)}, u32[]{:S(2)}) collective-permute-start(bf16[2,256,768]{2,1,0:T(8,128)(2,1)S(1)} %grad.29.refs_0_), channel_id=1, source_target_pairs={{0,16},{1,17},{2,18},{3,19},{4,20},{5,21},{6,22},{7,23},{8,24},{9,... | collective-permute-start | bytes 2359304 | tf_op jit(solution)/shard_map/ppermute | solution.py:811
  309.5 70.6 %all-to-all-start.6 = ((bf16[4,2,64,2048]{3,2,1,0:T(8,128)(2,1)}), bf16[4,2,64,2048]{3,2,1,0:T(8,128)(2,1)}, u32[]{:S(2)}, u32[]{:S(2)}) async-start(bf16[4,2,64,2048]{3,2,1,0:T(8,128)(2,1)} %bitcast.21), calls=%async_computation.6 | async-start | bytes 4194304 | tf_op jit(solution)/shard_map/all_to_all | solution.py:823
  330.3 24.7 %copy-start.41 = (f32[64,256]{1,0:T(8,128)}, f32[64,256]{1,0:T(8,128)S(1)}, u32[]{:S(2)}) copy-start(f32[64,256]{1,0:T(8,128)S(1)} %get-tuple-element.95) | copy-start | bytes 196612
  340.2 81.1 %copy-start.6 = (bf16[2,256,768]{2,1,0:T(8,128)(2,1)}, bf16[2,256,768]{2,1,0:T(8,128)(2,1)S(1)}, u32[]{:S(2)}) copy-start(bf16[2,256,768]{2,1,0:T(8,128)(2,1)S(1)} %collective-permute-done.15.refs_6_) | copy-start | bytes 2359300
  340.2 14.7 %collective-permute-start.16 = (bf16[2,512,128]{2,1,0:T(8,128)(2,1)S(1)}, bf16[2,512,128]{2,1,0:T(8,128)(2,1)S(1)}, u32[]{:S(2)}, u32[]{:S(2)}) collective-permute-start(bf16[2,512,128]{2,1,0:T(8,128)(2,1)S(1)} %get-tuple-element.85), channel_id=1, source_target_pairs={{0,4},{1,5},{2,6},{3,7},{4,0},{5,1},{6,2},{7,3},{8,12},{9,13},{10,... | collective-permute-start | bytes 786440 | tf_op jit(solution)/shard_map/ppermute | solution.py:811
  341.8 24.3 %collective-permute-start.17 = (bf16[2,512,128]{2,1,0:T(8,128)(2,1)S(1)}, bf16[2,512,128]{2,1,0:T(8,128)(2,1)S(1)}, u32[]{:S(2)}, u32[]{:S(2)}) collective-permute-start(bf16[2,512,128]{2,1,0:T(8,128)(2,1)S(1)} %get-tuple-element.86), channel_id=1, source_target_pairs={{0,16},{1,17},{2,18},{3,19},{4,20},{5,21},{6,22},{7,23},{8,24},{9,... | collective-permute-start | bytes 786440 | tf_op jit(solution)/shard_map/ppermute | solution.py:811
  347.7 24.4 %collective-permute-start.18 = (bf16[2,512,128]{2,1,0:T(8,128)(2,1)S(1)}, bf16[2,512,128]{2,1,0:T(8,128)(2,1)S(1)}, u32[]{:S(2)}, u32[]{:S(2)}) collective-permute-start(bf16[2,512,128]{2,1,0:T(8,128)(2,1)S(1)} %get-tuple-element.87), channel_id=1, source_target_pairs={{0,20},{1,21},{2,22},{3,23},{4,16},{5,17},{6,18},{7,19},{8,28},{9,... | collective-permute-start | bytes 786440 | tf_op jit(solution)/shard_map/ppermute | solution.py:811
  349.1 23.0 %copy-start.35 = (f32[64,1]{1,0:T(8,128)S(1)}, f32[64,1]{1,0:T(8,128)}, u32[]{:S(2)}) copy-start(f32[64,1]{1,0:T(8,128)} %copy-done.34) | copy-start | bytes 772
  380.1 4.5 collective-permute-start.19
  388.7 58.3 %all-to-all-start.7 = ((bf16[4,2,64,2048]{3,2,1,0:T(8,128)(2,1)}), bf16[4,2,64,2048]{3,2,1,0:T(8,128)(2,1)}, u32[]{:S(2)}, u32[]{:S(2)}) async-start(bf16[4,2,64,2048]{3,2,1,0:T(8,128)(2,1)} %bitcast.32), calls=%async_computation.7 | async-start | bytes 4194304 | tf_op jit(solution)/shard_map/all_to_all | solution.py:823
  397.6 48.8 %collective-permute-start.20 = (bf16[2,256,1024]{2,1,0:T(8,128)(2,1)S(1)}, bf16[2,256,1024]{2,1,0:T(8,128)(2,1)S(1)}, u32[]{:S(2)}, u32[]{:S(2)}) collective-permute-start(bf16[2,256,1024]{2,1,0:T(8,128)(2,1)S(1)} %grad.30.refs_0_), channel_id=1, source_target_pairs={{0,16},{1,17},{2,18},{3,19},{4,20},{5,21},{6,22},{7,23},{8,24},{9,... | collective-permute-start | bytes 3145736 | tf_op jit(solution)/shard_map/ppermute | solution.py:811
  405.6 70.7 %collective-permute-start.25 = (bf16[4,256,640]{2,1,0:T(8,128)(2,1)}, bf16[4,256,640]{2,1,0:T(8,128)(2,1)}, u32[]{:S(2)}, u32[]{:S(2)}) collective-permute-start(bf16[4,256,640]{2,1,0:T(8,128)(2,1)} %grad.31.refs_0_), channel_id=1, source_target_pairs={{0,4},{1,5},{2,6},{3,7},{4,0},{5,1},{6,2},{7,3},{8,12},{9,13},{10,... | collective-permute-start | bytes 3932168 | tf_op jit(solution)/shard_map/ppermute | solution.py:811
  410.9 43.6 %collective-permute-start.23 = (bf16[4,256,384]{2,1,0:T(8,128)(2,1)}, bf16[4,256,384]{2,1,0:T(8,128)(2,1)}, u32[]{:S(2)}, u32[]{:S(2)}) collective-permute-start(bf16[4,256,384]{2,1,0:T(8,128)(2,1)} %grad.32.refs_0_), channel_id=1, source_target_pairs={{0,4},{1,5},{2,6},{3,7},{4,0},{5,1},{6,2},{7,3},{8,12},{9,13},{10,... | collective-permute-start | bytes 2359304 | tf_op jit(solution)/shard_map/ppermute | solution.py:811
  421.0 97.9 %collective-permute-start.31 = (bf16[2,256,384]{2,1,0:T(8,128)(2,1)}, bf16[2,256,384]{2,1,0:T(8,128)(2,1)S(1)}, u32[]{:S(2)}, u32[]{:S(2)}) collective-permute-start(bf16[2,256,384]{2,1,0:T(8,128)(2,1)} %grad.34.refs_0_), channel_id=1, source_target_pairs={{0,4},{1,5},{2,6},{3,7},{4,0},{5,1},{6,2},{7,3},{8,12},{9,13},{10,... | collective-permute-start | bytes 1179656 | tf_op jit(solution)/shard_map/ppermute | solution.py:811
  421.4 3.9 collective-permute-start.21
  425.3 21.8 %copy-start.38 = (f32[33,128]{1,0:T(8,128)}, f32[33,128]{1,0:T(8,128)S(1)}, u32[]{:S(2)}) copy-start(f32[33,128]{1,0:T(8,128)S(1)} %collective-permute-done.21.refs_2_) | copy-start | bytes 50692
  425.3 47.5 %collective-permute-start.24 = (bf16[4,256,256]{2,1,0:T(8,128)(2,1)}, bf16[4,256,256]{2,1,0:T(8,128)(2,1)}, u32[]{:S(2)}, u32[]{:S(2)}) collective-permute-start(bf16[4,256,256]{2,1,0:T(8,128)(2,1)} %grad.33.refs_0_), channel_id=1, source_target_pairs={{0,4},{1,5},{2,6},{3,7},{4,0},{5,1},{6,2},{7,3},{8,12},{9,13},{10,... | collective-permute-start | bytes 1572872 | tf_op jit(solution)/shard_map/ppermute | solution.py:811
  446.4 38.5 %collective-permute-start.26 = (bf16[1,256,1024]{2,1,0:T(8,128)(2,1)}, bf16[1,256,1024]{2,1,0:T(8,128)(2,1)}, u32[]{:S(2)}, u32[]{:S(2)}) collective-permute-start(bf16[1,256,1024]{2,1,0:T(8,128)(2,1)} %grad.35.refs_0_), channel_id=1, source_target_pairs={{0,8},{1,9},{2,10},{3,11},{4,12},{5,13},{6,14},{7,15},{8,0},{9,1},... | collective-permute-start | bytes 1572872 | tf_op jit(solution)/shard_map/ppermute | solution.py:811
  454.0 20.1 %copy-start.24 = (bf16[4,2,64,256]{3,2,1,0:T(8,128)(2,1)S(1)}, bf16[4,2,64,256]{3,2,1,0:T(8,128)(2,1)}, u32[]{:S(2)}) copy-start(bf16[4,2,64,256]{3,2,1,0:T(8,128)(2,1)} %copy-done.22) | copy-start | bytes 786436
  454.0 20.1 %copy-start.28 = (bf16[4,2,64,256]{3,2,1,0:T(8,128)(2,1)S(1)}, bf16[4,2,64,256]{3,2,1,0:T(8,128)(2,1)}, u32[]{:S(2)}) copy-start(bf16[4,2,64,256]{3,2,1,0:T(8,128)(2,1)} %copy-done.26) | copy-start | bytes 786436
  454.5 37.6 %collective-permute-start.22 = (f32[33,128]{1,0:T(8,128)S(1)}, f32[33,128]{1,0:T(8,128)S(1)}, u32[]{:S(2)}, u32[]{:S(2)}) collective-permute-start(f32[33,128]{1,0:T(8,128)S(1)} %bitcast_add_fusion), channel_id=1, source_target_pairs={{0,2},{1,3},{2,0},{3,1},{4,6},{5,7},{6,4},{7,5},{8,10},{9,11},{10,... | collective-permute-start | bytes 50696 | tf_op jit(solution)/shard_map/ppermute | solution.py:811
  472.8 35.4 %collective-permute-start.27 = (bf16[2,256,384]{2,1,0:T(8,128)(2,1)S(1)}, bf16[2,256,384]{2,1,0:T(8,128)(2,1)S(1)}, u32[]{:S(2)}, u32[]{:S(2)}) collective-permute-start(bf16[2,256,384]{2,1,0:T(8,128)(2,1)S(1)} %grad.36.refs_0_), channel_id=1, source_target_pairs={{0,16},{1,17},{2,18},{3,19},{4,20},{5,21},{6,22},{7,23},{8,24},{9,... | collective-permute-start | bytes 1179656 | tf_op jit(solution)/shard_map/ppermute | solution.py:811
  480.0 48.1 %collective-permute-start.30 = (bf16[2,256,640]{2,1,0:T(8,128)(2,1)S(1)}, bf16[2,256,640]{2,1,0:T(8,128)(2,1)S(1)}, u32[]{:S(2)}, u32[]{:S(2)}) collective-permute-start(bf16[2,256,640]{2,1,0:T(8,128)(2,1)S(1)} %grad.38.refs_0_), channel_id=1, source_target_pairs={{0,16},{1,17},{2,18},{3,19},{4,20},{5,21},{6,22},{7,23},{8,24},{9,... | collective-permute-start | bytes 1966088 | tf_op jit(solution)/shard_map/ppermute | solution.py:811
  484.9 29.4 %collective-permute-start.29 = (bf16[1,256,1024]{2,1,0:T(8,128)(2,1)S(1)}, bf16[1,256,1024]{2,1,0:T(8,128)(2,1)S(1)}, u32[]{:S(2)}, u32[]{:S(2)}) collective-permute-start(bf16[1,256,1024]{2,1,0:T(8,128)(2,1)S(1)} %grad.39.refs_0_), channel_id=1, source_target_pairs={{0,8},{1,9},{2,10},{3,11},{4,12},{5,13},{6,14},{7,15},{8,0},{9,1},... | collective-permute-start | bytes 1572872 | tf_op jit(solution)/shard_map/ppermute | solution.py:811
  510.3 3.8 collective-permute-start.28
  510.3 21.1 %collective-permute-start.32 = (bf16[2,256,256]{2,1,0:T(8,128)(2,1)S(1)}, bf16[2,256,256]{2,1,0:T(8,128)(2,1)S(1)}, u32[]{:S(2)}, u32[]{:S(2)}) collective-permute-start(bf16[2,256,256]{2,1,0:T(8,128)(2,1)S(1)} %grad.37.refs_0_), channel_id=1, source_target_pairs={{0,16},{1,17},{2,18},{3,19},{4,20},{5,21},{6,22},{7,23},{8,24},{9,... | collective-permute-start | bytes 786440 | tf_op jit(solution)/shard_map/ppermute | solution.py:811
  514.1 21.2 %collective-permute-start.33 = (bf16[1,256,384]{2,1,0:T(8,128)(2,1)S(1)}, bf16[1,256,384]{2,1,0:T(8,128)(2,1)S(1)}, u32[]{:S(2)}, u32[]{:S(2)}) collective-permute-start(bf16[1,256,384]{2,1,0:T(8,128)(2,1)S(1)} %grad.41.refs_0_), channel_id=1, source_target_pairs={{0,8},{1,9},{2,10},{3,11},{4,12},{5,13},{6,14},{7,15},{8,0},{9,1},... | collective-permute-start | bytes 589832 | tf_op jit(solution)/shard_map/ppermute | solution.py:811
  531.2 18.2 %collective-permute-start.36 = (bf16[1,256,1024]{2,1,0:T(8,128)(2,1)S(1)}, bf16[1,256,1024]{2,1,0:T(8,128)(2,1)S(1)}, u32[]{:S(2)}, u32[]{:S(2)}) collective-permute-start(bf16[1,256,1024]{2,1,0:T(8,128)(2,1)S(1)} %grad.43.refs_0_), channel_id=1, source_target_pairs={{0,8},{1,9},{2,10},{3,11},{4,12},{5,13},{6,14},{7,15},{8,0},{9,1},... | collective-permute-start | bytes 1572872 | tf_op jit(solution)/shard_map/ppermute | solution.py:811
  533.4 13.3 %collective-permute-start.35 = (bf16[1,256,256]{2,1,0:T(8,128)(2,1)S(1)}, bf16[1,256,256]{2,1,0:T(8,128)(2,1)S(1)}, u32[]{:S(2)}, u32[]{:S(2)}) collective-permute-start(bf16[1,256,256]{2,1,0:T(8,128)(2,1)S(1)} %grad.44.refs_0_), channel_id=1, source_target_pairs={{0,8},{1,9},{2,10},{3,11},{4,12},{5,13},{6,14},{7,15},{8,0},{9,1},... | collective-permute-start | bytes 393224 | tf_op jit(solution)/shard_map/ppermute | solution.py:811
  538.3 5.0 collective-permute-start.34
  555.0 4.7 collective-permute-start.37
  (61 other events, 233.2 us)
